TPU v7x, 128 devices: a whole 4x4x4 slice. The times are simulated.
128 devices in a mesh: grp: 4 (over x_hi, core), chol: 32 (over y, x_lo, z).
Axes of the slice: x: 4 (x_hi: 2, x_lo: 2; x = x_hi * 2 + x_lo), y: 4, z: 4, core: 2. Of those that a mesh axis runs over, the one named last changes fastest.
Arguments:
- green: bfloat16 [1024, 2, 16, 128], P('chol', None, 'grp'), may hold values from -0.23925781 to 0.23925781
- chol_blocks: bfloat16 [8192, 128, 128], P(('grp', 'chol')), may hold values from -0.119628906 to 0.119628906
- block_ids: int32 [8192, 2], P(('grp', 'chol')), may hold values from 0 to 15, all different within a row
- noise: float32 [16, 8192], P(None, ('grp', 'chol')), may hold values from -6 to 6
- weights: float32 [16], P('grp'), may hold values from 0.5 to 2
- copies: int32 [16], P('grp'), may hold values from 0 to 4, as said below
- owners: int32 [16, 4], P('grp'), may hold values from 0 to 3, as said below
Outputs:
- force_bias: float32 [2, 16, 8192], P(None, None, ('grp', 'chol'))
- energy: float32 [2, 16], P(None, 'grp')
- new_weights: float32 [16], P('grp')
- moved_green: bfloat16 [1024, 2, 16, 128], P('chol', None, 'grp')
- moved_weights: float32 [16], P('grp')
Inputs may be any that keep to these rules, and one draw needn't show every extreme that they name: The copies of all walkers sum to 16; some walker has 4 copies and some have none. `owners`: over the live entries (j < copies[w]) every task group is named exactly 4 times; entries with j >= copies[w] are ignored. `block_ids`: each vector names 2 different orbital blocks.
All inputs are finite; a program needn't handle non-finite values.
Results may differ from a plain program's by a relative error of at most 0.011.
The roundings to bfloat16 on the way count: a program that leaves them out, or rounds other values in their place, can miss the bound.
Values may be sent and summed in bfloat16 or wider, within the bound.
A program may use at most 64 MiB of HBM per device.

v0:
```python
import math

import jax
import jax.numpy as jnp
from jax import lax
from jax.sharding import PartitionSpec as P

BLOCK = 64
KMAX = 4
RW = 2


time_step = 0.005


def block_size(total, per_item, limit):
    best = 1
    for candidate in range(1, total + 1):
        if total % candidate == 0 and candidate * per_item <= limit:
            best = candidate
    return best


def contract(blocks, ids, stacked, fields):
    groups, orbitals, pairs, walkers, electrons = stacked.shape
    cols = walkers * pairs * electrons
    reordered = jnp.transpose(stacked, (0, 1, 3, 2, 4))
    flat = reordered.reshape(groups, orbitals // BLOCK, BLOCK, cols)
    vector_count = blocks.shape[0]
    width = blocks.shape[2]
    size = block_size(vector_count, electrons * groups * cols, 2**20)
    block_total = vector_count // size
    identity = jnp.eye(electrons, dtype=jnp.bfloat16)
    identity_wide = jnp.eye(electrons, dtype=jnp.float32)
    root = math.sqrt(time_step)

    def square_trace(left, right):
        square = jnp.einsum("vgwei,vgwik->vgwek", left, right, preferred_element_type=jnp.float32)
        return jnp.transpose(jnp.sum(square * identity_wide, axis=(3, 4)), (1, 2, 0))

    def one_block(items):
        part_blocks, part_ids, part_fields = items
        selected = jnp.take(flat, part_ids, axis=1).reshape(groups, size, width, cols)
        product = jnp.einsum(
            "vik,gvkx->vgxi", part_blocks, selected, preferred_element_type=jnp.float32
        ).astype(jnp.bfloat16)
        product = product.reshape(size, groups, walkers, pairs, electrons, electrons)
        diagonal = jnp.einsum(
            "vgwcei,ei->vgwc", product, identity, preferred_element_type=jnp.float32
        )
        traces = 2.0 * jnp.transpose(diagonal, (3, 1, 2, 0))
        real_part = product[:, :, :, 0]
        imag_part = product[:, :, :, 1]
        real_real = square_trace(real_part, real_part)
        imag_imag = square_trace(imag_part, imag_part)
        real_imag = square_trace(real_part, imag_part)
        bias_real = traces[0]
        bias_imag = traces[1]
        energy_real = 0.5 * (bias_real * bias_real - bias_imag * bias_imag) - (
            real_real - imag_imag
        )
        energy_imag = bias_real * bias_imag - 2.0 * real_imag
        shift_real = -root * bias_real
        shift_imag = -root * bias_imag
        phase_real = part_fields * shift_real - 0.5 * (
            shift_real * shift_real - shift_imag * shift_imag
        )
        phase_imag = part_fields * shift_imag - shift_real * shift_imag
        energy = jnp.stack([jnp.sum(energy_real, axis=2), jnp.sum(energy_imag, axis=2)])
        phase = jnp.stack([jnp.sum(phase_real, axis=2), jnp.sum(phase_imag, axis=2)])
        return (traces, energy, phase)

    blocks_in = blocks.reshape(block_total, size, electrons, width)
    ids_in = ids.reshape(block_total, size, ids.shape[1])
    fields_in = jnp.moveaxis(fields.reshape(groups, walkers, block_total, size), 2, 0)
    traces, energies, phases = lax.map(one_block, (blocks_in, ids_in, fields_in))
    bias = jnp.moveaxis(traces, 0, 3).reshape(2, groups, walkers, vector_count)
    return (bias, jnp.sum(energies, axis=0), jnp.sum(phases, axis=0))


def body(green, chol_blocks, block_ids, noise, weights, copies, owners):
    groups = lax.axis_size("grp")
    walkers_group = weights.shape[0]
    walker_total = groups * walkers_group
    rounds = walkers_group // RW
    local_vectors = chol_blocks.shape[0]
    electrons = green.shape[3]
    all_copies, all_owners = (
        lax.all_gather(copies, "grp", axis=0, tiled=True),
        lax.all_gather(owners, "grp", axis=0, tiled=True),
    )
    kept = jnp.arange(KMAX, dtype=jnp.int32)[None, :] < all_copies[:, None]
    targets = jnp.arange(groups, dtype=jnp.int32)
    hits = ((all_owners[:, :, None] == targets[None, None, :]) & kept[:, :, None]).astype(jnp.int32)
    hits = hits.reshape(walker_total * KMAX, groups)
    ranks = jnp.cumsum(hits, axis=0, dtype=jnp.int32) - hits
    slots = jnp.sum(hits * (ranks + targets[None, :] * walkers_group), axis=1, dtype=jnp.int32)
    live = jnp.sum(hits, axis=1, dtype=jnp.int32) > 0
    own_slots = lax.axis_index("grp") * walkers_group + jnp.arange(walkers_group, dtype=jnp.int32)
    route = ((slots[:, None] == own_slots[None, :]) & live[:, None]).astype(jnp.float32)
    route = jnp.sum(route.reshape(walker_total, KMAX, walkers_group), axis=1)
    bias_parts = []
    energy_parts = []
    phase_parts = []
    local_fields = noise.reshape(groups, walkers_group, local_vectors)
    for turn in range(rounds):
        local = green[:, :, turn * RW : (turn + 1) * RW, :]
        stacked = lax.all_gather(local[None], ("grp", "chol"), axis=0, tiled=True)
        stacked = stacked.reshape(groups, -1, 2, RW, electrons)
        bias, energy_term, phase_term = contract(
            chol_blocks, block_ids, stacked, local_fields[:, turn * RW : (turn + 1) * RW, :]
        )
        bias_parts.append(bias)
        energy_parts.append(energy_term)
        phase_parts.append(phase_term)
    force_bias = jnp.stack(bias_parts, axis=2).reshape(2, walker_total, local_vectors)
    energy_all = jnp.stack(energy_parts, axis=2).reshape(2, walker_total)
    phase_all = jnp.stack(phase_parts, axis=2).reshape(2, walker_total)
    energy_all, phase_all = lax.psum((energy_all, phase_all), ("grp", "chol"))
    start = lax.axis_index("grp") * walkers_group
    energy = lax.dynamic_slice_in_dim(energy_all, start, walkers_group, axis=1)
    phase = lax.dynamic_slice_in_dim(phase_all, start, walkers_group, axis=1)
    new_weights = weights * jnp.exp(phase[0]) * jnp.maximum(jnp.cos(phase[1]), 0.0)
    every_green, every_weight = (
        lax.all_gather(green, "grp", axis=2, tiled=True),
        lax.all_gather(new_weights.astype(jnp.bfloat16), "grp", axis=0, tiled=True).astype(
            new_weights.dtype
        ),
    )
    moved_green = jnp.einsum(
        "mcwn,ws->mcsn", every_green, route.astype(jnp.bfloat16), preferred_element_type=jnp.float32
    ).astype(jnp.bfloat16)
    moved_weights = jnp.sum(route * every_weight[:, None], axis=0)
    return (force_bias, energy, new_weights, moved_green, moved_weights)


def solution(mesh):
    return jax.shard_map(
        body,
        mesh=mesh,
        in_specs=(
            P("chol", None, "grp", None),
            P(("grp", "chol"), None, None),
            P(("grp", "chol"), None),
            P(None, ("grp", "chol")),
            P("grp"),
            P("grp"),
            P("grp", None),
        ),
        out_specs=(
            P(None, None, ("grp", "chol")),
            P(None, "grp"),
            P("grp"),
            P("chol", None, "grp", None),
            P("grp"),
        ),
        check_vma=False,
    )
```

profile of v0, /device:TPU:1, one launch (start us, length us, event | category | flops | bytes accessed | tf_op | source)
XLA Modules:
  0.0 936.6 jit_solution(60578502681162001)
XLA Ops:
  12.2 8.6 all_gather.22
  20.8 6.7 all-gather.2
  30.4 5.6 all-reduce
  38.0 281.0 %all-gather.8.cloned.1.call-done = bf16[4096,2,2,128]{3,2,1,0:T(2,128)(2,1)} async-done(((bf16[32,2,2,128]{3,2,1,0:T(2,128)(2,1)}), bf16[4096,2,2,128]{3,2,1,0:T(2,128)(2,1)}) %all-gather.8.cloned.1.call-update) | async-done | bytes 4194320 | tf_op jit(solution)/shard_map/all_gather | solution.py:108
  319.0 7.0 copy.195
  326.0 7.2 reshape.174
  333.3 214.4 %while.33 = (s32[]{:T(128)}, f32[16,2,4,2,4]{4,3,2,1,0:T(2,128)S(1)}, f32[16,2,4,2]{2,3,1,0:T(2,128)S(1)}, f32[16,2,4,2]{2,3,1,0:T(2,128)S(1)}, s32[16,4,2]{1,2,...) while((s32[]{:T(128)}, ...), condition=%wide.region_17.19_spmd.clone.clone, body=%wide.region_9.18_spmd.clone.clone.sunk | while | flops 678496128 | bytes 23560728 | solution.py:76
  333.6 4.3 gather_fusion.1
  341.8 2.2 fusion.106
  347.0 4.3 gather_fusion.1
  355.2 2.2 fusion.106
  360.4 4.3 gather_fusion.1
  368.6 2.2 fusion.106
  373.8 4.3 gather_fusion.1
  382.0 2.2 fusion.106
  387.2 4.3 gather_fusion.1
  395.4 2.2 fusion.106
  400.6 4.3 gather_fusion.1
  408.8 2.2 fusion.106
  414.0 4.3 gather_fusion.1
  422.2 2.2 fusion.106
  427.4 4.3 gather_fusion.1
  435.6 2.2 fusion.106
  440.8 4.3 gather_fusion.1
  449.0 2.2 fusion.106
  454.2 4.3 gather_fusion.1
  462.4 2.2 fusion.106
  467.6 4.3 gather_fusion.1
  475.8 2.2 fusion.106
  481.0 4.3 gather_fusion.1
  489.2 2.2 fusion.106
  494.4 4.3 gather_fusion.1
  502.6 2.2 fusion.106
  507.8 4.3 gather_fusion.1
  516.0 2.2 fusion.106
  521.2 4.3 gather_fusion.1
  529.4 2.2 fusion.106
  534.6 4.3 gather_fusion.1
  542.8 2.2 fusion.106
  547.9 77.0 %all-gather.6.cloned.1.call-done = bf16[4096,2,2,128]{3,2,1,0:T(2,128)(2,1)} async-done(((bf16[32,2,2,128]{3,2,1,0:T(2,128)(2,1)}), bf16[4096,2,2,128]{3,2,1,0:T(2,128)(2,1)}) %all-gather.6.cloned.1.call-update) | async-done | bytes 4194320 | tf_op jit(solution)/shard_map/all_gather | solution.py:108
  624.9 7.0 copy.191
  632.0 7.2 reshape.169
  639.3 213.5 %while.32 = (s32[]{:T(128)}, f32[16,2,4,2,4]{4,3,2,1,0:T(2,128)S(1)}, f32[16,2,4,2]{2,3,1,0:T(2,128)S(1)}, f32[16,2,4,2]{2,3,1,0:T(2,128)S(1)}, s32[16,4,2]{1,2,...) while((s32[]{:T(128)}, ...), condition=%wide.region_8.10_spmd.clone.clone, body=%wide.region_0.9_spmd.clone.clone.sunk | while | flops 678496128 | bytes 23560728 | solution.py:76
  639.7 4.2 gather_fusion
  647.8 2.2 fusion.94
  653.0 4.2 gather_fusion
  666.4 4.2 gather_fusion
  679.7 4.2 gather_fusion
  693.0 4.2 gather_fusion
  706.3 4.2 gather_fusion
  719.7 4.2 gather_fusion
  733.0 4.2 gather_fusion
  746.3 4.2 gather_fusion
  759.7 4.2 gather_fusion
  773.0 4.2 gather_fusion
  786.3 4.2 gather_fusion
  799.7 4.2 gather_fusion
  807.8 2.2 fusion.94
  813.0 4.2 gather_fusion
  826.3 4.2 gather_fusion
  839.7 4.2 gather_fusion
  847.8 2.2 fusion.94
  853.5 66.2 %all-reduce.2 = (f32[2,16]{1,0:T(2,128)S(1)}, f32[2,16]{1,0:T(2,128)S(1)}) all-reduce(f32[2,16]{1,0:T(2,128)S(1)} %reshape.177, f32[2,16]{1,0:T(2,128)S(1)} %reshape.178), channel_id=1, replica_groups=mesh['grp'=4,'chol'=32] {'grp','chol'}, use_global_device_ids=true, to_apply=%region_20.22 | all-reduce | flops 64 | bytes 512 | tf_op jit(solution)/shard_map/psum | solution.py:119
  921.8 7.4 all-reduce.1
  (905 shorter events, 260.1 us)
Async XLA Ops:
  7.2 311.8 %all-gather.8.cloned.1.call-start = ((), (), s32[]{:S(2)}) async-start(), calls=%async_computation.1 | async-start | bytes 4227072 | tf_op jit(solution)/shard_map/all_gather | solution.py:108
  8.8 616.1 %all-gather.6.cloned.1.call-start = ((), (), s32[]{:S(2)}) async-start(), calls=%async_computation | async-start | bytes 4227072 | tf_op jit(solution)/shard_map/all_gather | solution.py:108
  639.2 281.2 %copy-start = (f32[4]{0:T(128)S(1)}, f32[4]{0:T(128)}, u32[]{:S(2)}) copy-start(f32[4]{0:T(128)} %param.17) | copy-start | bytes 52
Sparse Core Ops, SparseCore 0:
  9.7 309.2 all-gather.7
  320.7 304.1 all-gather.5
where the time goes:
time: 940 us; the launch traced here: 937 us
  waiting for transfers between devices  359 us (38%)
  local copies, waits for them, and re-layouts  262 us (28%)
  matrix products  183 us (19%)
  blocking collectives  94.5 us (10%)
  other arithmetic  20.8 us (2%)
  between operations  14.9 us (2%)
    all_gather x2, waiting for transfers between devices, body(): stacked = lax.all_gather(local[None], ('grp', 'chol'), axis=0, tiled=True)  358 us
    gather x64, local copies, waits for them, and re-layouts, one_block(): jnp.take(flat, part_ids, axis=1).reshape(groups, size, width, cols)  192 us
    dot_general x32, matrix products, one_block(): jnp.einsum('vgwcei,ei->vgwc', product, identity, preferred_element_type=j...  71.6 us
    psum x1, blocking collectives, body(): energy_all, phase_all = lax.psum((energy_all, phase_all), ('grp', 'chol'))  66.2 us
    dot_general x32, matrix products, one_block(): jnp.einsum('vik,gvkx->vgxi', part_blocks, selected, preferred_element_typ...  57.5 us
    dot_general x96, matrix products, square_trace(): jnp.einsum('vgwei,vgwik->vgwek', left, right, preferred_element_type=jnp....  52.6 us
  transfers between devices with their start and end apart: 2, of which 2 were waited for; matrix products, arithmetic and copies ran while one was open for 25% of the time, Pallas kernels for 0%

commit v1 on v0

v1 whole, which is shorter than its diff:
```python
import functools
import math

import jax
import jax.numpy as jnp
from jax import lax
from jax.experimental import pallas as pl
from jax.experimental.pallas import tpu as pltpu
from jax.sharding import PartitionSpec as P

MESH = pl.DeviceIdType.MESH
BF16 = jnp.bfloat16
F32 = jnp.float32
KMAX = 4
GROUPS = 4
WG = 4
ROOT = math.sqrt(0.005)
MB = 2**20

STREAMS = (
    (0, 0, 2, "xyz"),
    (1, 0, 2, "yzx"),
    (2, 0, 2, "zxy"),
    (3, 0, 1, "xyz"),
    (3, 1, 1, "yzx"),
)


def position():
    grp = lax.axis_index("grp")
    chol = lax.axis_index("chol")
    x = (grp // 2) * 2 + (chol // 4) % 2
    return x, chol // 8, chol % 4, grp % 2


def device(x, y, z, core):
    return ((x // 2) * 2 + core, y * 8 + (x % 2) * 4 + z)


def gather_kernel(
    shard, vectors, ids, noise, meta, green,
    gathered, vectors2, ids2, noise2, meta_all, green_all,
    local_sem, send_sem, recv_sem, pair_send, pair_recv, group_send, group_recv,
):
    x, y, z, core = position()
    grp = lax.axis_index("grp")
    here = {"x": x, "y": y, "z": z}
    sibling = device(x, y, z, 1 - core)
    across = [device((x + 2) % 4, y, z, core), device((x + 2) % 4, y, z, 1 - core)]
    neighbours = []
    for axis in "xyz":
        for step in (1, 3):
            there = dict(here)
            there[axis] = (here[axis] + step) % 4
            neighbours.append(device(there["x"], there["y"], there["z"], core))
    barrier = pltpu.get_barrier_semaphore()
    everyone = neighbours + [sibling] + across
    for target in everyone:
        pl.semaphore_signal(barrier, inc=1, device_id=target, device_id_type=MESH)

    local = [
        pltpu.make_async_copy(shard, gathered.at[:, x, y, z], local_sem.at[0]),
        pltpu.make_async_copy(meta, meta_all.at[grp], local_sem.at[1]),
        pltpu.make_async_copy(green, green_all.at[grp], local_sem.at[2]),
    ]
    for copy in local:
        copy.start()
    pl.semaphore_wait(barrier, len(everyone))

    def remote(source, target, send, recv, where):
        return pltpu.make_async_remote_copy(
            src_ref=source, dst_ref=target, send_sem=send, recv_sem=recv,
            device_id=where, device_id_type=MESH,
        )

    others = [
        remote(ids, ids2, pair_send.at[0], pair_recv.at[0], sibling),
        remote(noise, noise2, pair_send.at[1], pair_recv.at[1], sibling),
        remote(vectors, vectors2, pair_send.at[2], pair_recv.at[2], sibling),
    ]
    for i, target in enumerate([sibling] + across):
        others.append(remote(meta, meta_all.at[grp], group_send.at[0, i], group_recv.at[0, i], target))
        others.append(remote(green, green_all.at[grp], group_send.at[1, i], group_recv.at[1, i], target))

    def view(stream, free, at, rows):
        walker, first, count, _ = STREAMS[stream]
        index = [slice(None) if axis in free else at[axis] for axis in "xyz"]
        return gathered.at[
            (walker, *index, pl.ds(rows[0], rows[1]), pl.ds(first * 128, count * 128))
        ]

    local[0].wait()
    pending = [[] for _ in STREAMS]
    for phase in range(3):
        moves = []
        for stream, (_, _, _, order) in enumerate(STREAMS):
            for copy in pending[stream]:
                copy.wait()
            axis, free = order[phase], order[:phase]
            up, down = dict(here), dict(here)
            up[axis] = (here[axis] + 1) % 4
            down[axis] = (here[axis] + 3) % 4
            to_up = device(up["x"], up["y"], up["z"], core)
            to_down = device(down["x"], down["y"], down["z"], core)

            def make(kind, at, rows, target):
                part = view(stream, free, at, rows)
                return remote(
                    part, part, send_sem.at[stream, phase, kind], recv_sem.at[stream, phase, kind], target
                )

            first = [make(0, here, (0, 32), to_up), make(1, here, (0, 32), to_down)]
            second = [make(2, down, (0, 16), to_up), make(3, up, (16, 16), to_down)]
            for copy in first:
                copy.start()
            moves.append((first, second))
        if phase == 0:
            for copy in others:
                copy.start()
        for first, second in moves:
            for one, two in zip(first, second):
                one.wait_recv()
                two.start()
        for stream, (first, second) in enumerate(moves):
            for copy in first:
                copy.wait_send()
            pending[stream] = second
    for copies in pending:
        for copy in copies:
            copy.wait()
    for copy in others:
        copy.wait()
    for copy in local[1:]:
        copy.wait()


def gather(shard, vectors, ids, noise, meta, green):
    spec = pl.BlockSpec(memory_space=pl.ANY)
    streams = len(STREAMS)
    shape = jax.ShapeDtypeStruct
    return pl.pallas_call(
        gather_kernel,
        out_shape=(
            shape((WG, 4, 4, 4) + shard.shape[1:], shard.dtype),
            shape(vectors.shape, vectors.dtype),
            shape(ids.shape, ids.dtype),
            shape(noise.shape, noise.dtype),
            shape((GROUPS,) + meta.shape, meta.dtype),
            shape((GROUPS,) + green.shape, green.dtype),
        ),
        in_specs=[spec] * 6,
        out_specs=(spec,) * 6,
        scratch_shapes=[
            pltpu.SemaphoreType.DMA((3,)),
            pltpu.SemaphoreType.DMA((streams, 3, 4)),
            pltpu.SemaphoreType.DMA((streams, 3, 4)),
            pltpu.SemaphoreType.DMA((3,)),
            pltpu.SemaphoreType.DMA((3,)),
            pltpu.SemaphoreType.DMA((2, 3)),
            pltpu.SemaphoreType.DMA((2, 3)),
        ],
        compiler_params=pltpu.CompilerParams(collective_id=0, has_side_effects=True),
        name="gather_green",
    )(shard, vectors, ids, noise, meta, green)


WALKERS_HERE = 8
CHUNK = 4


def diagonal(block, masks):
    merged = block[0:16]
    for r in range(1, 8):
        merged = jnp.where(masks[r], block[16 * r : 16 * r + 16], merged)
    return merged


def contract_kernel(ids_a, ids_b, vec_a, vec_b, green, noise, bias_ref, part_ref, acc, diag):
    vectors = vec_a.shape[0]
    acc[...] = jnp.zeros_like(acc)
    lane16 = lax.broadcasted_iota(jnp.int32, (16, 128), 1)
    masks = [(lane16 // 16) == r for r in range(8)]

    def half(ids, vec, offset):
        def step(turn, carry):
            for w in range(WALKERS_HERE):
                lefts, rights = [], []
                for k in range(CHUNK):
                    g = turn * CHUNK + k
                    rows = []
                    for j in range(2):
                        b = ids[2 * g + j]
                        rows.append(green[w % 4, (w // 4) * 2 + (b // 2) % 2, b // 4, b % 2])
                    tee = jnp.dot(
                        vec[g], jnp.concatenate(rows, 0), preferred_element_type=F32
                    ).astype(BF16)
                    real, imag = tee[:, :128], tee[:, 128:]
                    diag[w, 0, offset + g] = diagonal(real, masks)
                    diag[w, 1, offset + g] = diagonal(imag, masks)
                    lefts.append(tee)
                    rights += [tee, jnp.concatenate([-imag, real], 1)]
                acc[w] += jnp.dot(
                    jnp.concatenate(lefts, 1), jnp.concatenate(rights, 0), preferred_element_type=F32
                )
            return carry

        lax.fori_loop(0, vectors // CHUNK, step, 0)

    half(ids_a, vec_a, 0)
    half(ids_b, vec_b, vectors)

    total = 2 * vectors
    keep = (lax.broadcasted_iota(jnp.int32, (1, 16, 128), 2) % 16) == lax.broadcasted_iota(
        jnp.int32, (1, 16, 128), 1
    )
    block = 16
    span = lax.broadcasted_iota(jnp.int32, (block, block * 16), 1) // 16
    pick = (span == lax.broadcasted_iota(jnp.int32, (block, block * 16), 0)).astype(BF16)
    row16 = lax.broadcasted_iota(jnp.int32, (16, 128), 0)
    bias = jnp.zeros((16, total), F32)
    for w in range(WALKERS_HERE):
        for c in range(2):
            pieces = []
            for p in range(total // block):
                part = diag[w, c, p * block : (p + 1) * block]
                part = jnp.where(keep, part, jnp.zeros_like(part)).reshape(block * 16, 128)
                pieces.append(jnp.dot(pick, part, preferred_element_type=F32).astype(BF16))
            sums = jnp.concatenate(pieces, 0)
            ones = (row16 == c * 8 + w).astype(BF16)
            bias += lax.dot_general(ones, sums, (((1,), (1,)), ((), ())), preferred_element_type=F32)
    bias = 2.0 * bias
    bias_ref[...] = bias
    eye = lax.broadcasted_iota(jnp.int32, (128, 128), 0) == lax.broadcasted_iota(jnp.int32, (128, 128), 1)
    row8 = lax.broadcasted_iota(jnp.int32, (8, 128), 0)
    kx = [jnp.zeros((8, 128), F32), jnp.zeros((8, 128), F32)]
    for w in range(WALKERS_HERE):
        for c in range(2):
            square = acc[w, :, c * 128 : (c + 1) * 128]
            line = jnp.sum(jnp.where(eye, square, 0.0), axis=0, keepdims=True)
            kx[c] += jnp.where(row8 == w, line, 0.0)
    re, im = bias[:8], bias[8:]
    fields = noise[...]
    energy_re = 0.5 * (re * re - im * im) - kx[0]
    energy_im = re * im - kx[1]
    shift_re, shift_im = -ROOT * re, -ROOT * im
    phase_re = fields * shift_re - 0.5 * (shift_re * shift_re - shift_im * shift_im)
    phase_im = fields * shift_im - shift_re * shift_im
    lane8 = lax.broadcasted_iota(jnp.int32, (8, 128), 1)
    result = jnp.zeros((8, 128), F32)
    for i, value in enumerate((energy_re, energy_im, phase_re, phase_im)):
        result = jnp.where(lane8 == i, jnp.sum(value, axis=1, keepdims=True), result)
    part_ref[...] = result


def contract(ids_a, ids_b, vec_a, vec_b, green, noise):
    smem = pl.BlockSpec(memory_space=pltpu.SMEM)
    vmem = pl.BlockSpec(memory_space=pltpu.VMEM)
    vectors = vec_a.shape[0]
    return pl.pallas_call(
        contract_kernel,
        out_shape=(
            jax.ShapeDtypeStruct((16, 2 * vectors), F32),
            jax.ShapeDtypeStruct((8, 128), F32),
        ),
        in_specs=[smem, smem, vmem, vmem, vmem, vmem],
        out_specs=(vmem, vmem),
        scratch_shapes=[
            pltpu.VMEM((WALKERS_HERE, 128, 256), F32),
            pltpu.VMEM((WALKERS_HERE, 2, 2 * vectors, 16, 128), BF16),
        ],
        compiler_params=pltpu.CompilerParams(vmem_limit_bytes=56 * MB),
        name="tee_and_traces",
    )(ids_a, ids_b, vec_a, vec_b, green, noise)


def reduce_kernel(
    part, bias, total_ref, bias2_ref, slots, slots2, own2,
    bias_send, bias_recv, send_sem, recv_sem, send2, recv2,
):
    x, y, z, core = position()
    sibling = device(x, y, z, 1 - core)
    plane = [
        device((x + i) % 4, (y + j) % 4, z, core)
        for i in range(4) for j in range(4) if i + j > 0
    ]
    column = [
        device(x, y, (z + i) % 4, (core + k) % 2)
        for k in range(2) for i in range(4) if i + k > 0
    ]
    barrier = pltpu.get_barrier_semaphore()
    for target in plane + column:
        pl.semaphore_signal(barrier, inc=1, device_id=target, device_id_type=MESH)
    me = x * 4 + y
    me2 = core * 4 + z
    slots[me] = part[...]
    pl.semaphore_wait(barrier, len(plane) + len(column))

    def remote(source, target, send, recv, where):
        return pltpu.make_async_remote_copy(
            src_ref=source, dst_ref=target, send_sem=send, recv_sem=recv,
            device_id=where, device_id_type=MESH,
        )

    first = [
        remote(part, slots.at[me], send_sem.at[i], recv_sem.at[i], target)
        for i, target in enumerate(plane)
    ]
    for copy in first:
        copy.start()
    swap = remote(bias, bias2_ref, bias_send, bias_recv, sibling)
    swap.start()
    for copy in first:
        copy.wait()
    mine = jnp.sum(slots[...], axis=0)
    own2[...] = mine
    slots2[me2] = mine
    second = [
        remote(own2, slots2.at[me2], send2.at[i], recv2.at[i], target)
        for i, target in enumerate(column)
    ]
    for copy in second:
        copy.start()
    for copy in second:
        copy.wait()
    total_ref[0] = jnp.sum(slots2[0:4], axis=0)
    total_ref[1] = jnp.sum(slots2[4:8], axis=0)
    swap.wait()


def reduce_all(part, bias):
    vmem = pl.BlockSpec(memory_space=pltpu.VMEM)
    return pl.pallas_call(
        reduce_kernel,
        out_shape=(
            jax.ShapeDtypeStruct((2, 8, 128), F32),
            jax.ShapeDtypeStruct(bias.shape, F32),
        ),
        in_specs=[vmem, vmem],
        out_specs=(vmem, vmem),
        scratch_shapes=[
            pltpu.VMEM((16, 8, 128), F32),
            pltpu.VMEM((8, 8, 128), F32),
            pltpu.VMEM((8, 128), F32),
            pltpu.SemaphoreType.DMA(()),
            pltpu.SemaphoreType.DMA(()),
            pltpu.SemaphoreType.DMA((15,)),
            pltpu.SemaphoreType.DMA((15,)),
            pltpu.SemaphoreType.DMA((7,)),
            pltpu.SemaphoreType.DMA((7,)),
        ],
        compiler_params=pltpu.CompilerParams(collective_id=1, has_side_effects=True),
        name="reduce_terms",
    )(part, bias)


def body(green, chol_blocks, block_ids, noise, weights, copies, owners):
    grp = lax.axis_index("grp")
    core = grp % 2
    rows, _, _, electrons = green.shape
    vectors = chol_blocks.shape[0]
    shard = jnp.transpose(green, (2, 0, 1, 3)).reshape(WG, rows, 2 * electrons)
    ids = block_ids.reshape(-1)
    meta = jnp.concatenate(
        [weights[:, None], copies[:, None].astype(F32), owners.astype(F32)], axis=1
    )
    meta = jnp.pad(meta, ((0, 4), (0, 128 - 6)))
    gathered, vectors2, ids2, noise2, meta_all, green_all = gather(
        shard, chol_blocks, ids.reshape(1, -1), noise, meta, green
    )
    meta_all = meta_all[:, :WG].reshape(GROUPS * WG, -1)
    all_weights = meta_all[:, 0]
    all_copies = meta_all[:, 1].astype(jnp.int32)
    all_owners = meta_all[:, 2:6].astype(jnp.int32)
    kept = jnp.arange(KMAX, dtype=jnp.int32)[None, :] < all_copies[:, None]
    targets = jnp.arange(GROUPS, dtype=jnp.int32)
    hits = ((all_owners[:, :, None] == targets[None, None, :]) & kept[:, :, None]).astype(jnp.int32)
    hits = hits.reshape(GROUPS * WG * KMAX, GROUPS)
    ranks = jnp.cumsum(hits, axis=0, dtype=jnp.int32) - hits
    slots = jnp.sum(hits * (ranks + targets[None, :] * WG), axis=1, dtype=jnp.int32)
    live = jnp.sum(hits, axis=1, dtype=jnp.int32) > 0
    own_slots = grp * WG + jnp.arange(WG, dtype=jnp.int32)
    route = ((slots[:, None] == own_slots[None, :]) & live[:, None]).astype(F32)
    route = jnp.sum(route.reshape(GROUPS * WG, KMAX, WG), axis=1)
    moved_green = jnp.einsum(
        "gmcwn,gws->mcsn", green_all, route.reshape(GROUPS, WG, WG).astype(BF16),
        preferred_element_type=F32,
    ).astype(BF16)

    def mine(fields):
        return lax.dynamic_index_in_dim(
            fields.reshape(2, 2, WG, vectors), core, axis=1, keepdims=False
        ).reshape(WALKERS_HERE, vectors)

    fields = jnp.concatenate([mine(noise), mine(noise2)], axis=1)
    blocks = gathered.reshape(WG, 4, 4, 2, 2 * rows, 2 * electrons)
    bias, part = contract(ids, ids2.reshape(-1), chol_blocks, vectors2, blocks, fields)
    total, bias2 = reduce_all(part, bias)
    terms = jnp.transpose(total[:, :, :4].reshape(2, 2, WG, 4), (3, 1, 0, 2)).reshape(4, GROUPS * WG)
    every_weight = all_weights * jnp.exp(terms[2]) * jnp.maximum(jnp.cos(terms[3]), 0.0)
    energy = lax.dynamic_slice_in_dim(terms[:2], grp * WG, WG, axis=1)
    new_weights = lax.dynamic_slice_in_dim(every_weight, grp * WG, WG, axis=0)
    moved_weights = jnp.sum(route * every_weight[:, None], axis=0)
    ours = bias[:, :vectors].reshape(2, 2, WG, vectors)
    theirs = bias2[:, vectors:].reshape(2, 2, WG, vectors)
    force_bias = jnp.where(
        core == 0, jnp.stack([ours, theirs], axis=2), jnp.stack([theirs, ours], axis=2)
    ).reshape(2, GROUPS * WG, vectors)
    return (force_bias, energy, new_weights, moved_green, moved_weights)


def solution(mesh):
    return jax.shard_map(
        body,
        mesh=mesh,
        in_specs=(
            P("chol", None, "grp", None),
            P(("grp", "chol"), None, None),
            P(("grp", "chol"), None),
            P(None, ("grp", "chol")),
            P("grp"),
            P("grp"),
            P("grp", None),
        ),
        out_specs=(
            P(None, None, ("grp", "chol")),
            P(None, "grp"),
            P("grp"),
            P("chol", None, "grp", None),
            P("grp"),
        ),
        check_vma=False,
    )
```

time: 940 us -> 125 us (0.13)
  waiting for transfers between devices: 359 us -> 0 us
  local copies, waits for them, and re-layouts: 262 us -> 9.8 us
  matrix products: 183 us -> 1.06 us
  Pallas kernels: 0 us -> 108 us
  blocking collectives: 94.5 us -> 0 us
  other arithmetic: 20.8 us -> 4.86 us
  between operations: 14.9 us -> 0.76 us
    all_gather x2 -> x0, waiting for transfers between devices: 358 us -> none  [body(): stacked = lax.all_gather(local[None], ('grp', 'chol'), axis=0, tiled=True)]
    gather x64 -> x0, local copies, waits for them, and re-layouts: 192 us -> none  [one_block(): jnp.take(flat, part_ids, axis=1).reshape(groups, size, width, cols)]
    dot_general x161 -> x1, matrix products: 183 us -> 1.06 us  [body(): jnp.einsum('gmcwn,gws->mcsn', green_all, route.reshape(GROUPS, WG, WG).as...]
    pallas_call x0 -> x3, Pallas kernels: none -> 108 us  [the longest x1 54.8 us: contract(): pl.pallas_call(contract_kernel, out_shape=(jax.ShapeDtypeStruct((16, 2 *...]
    psum x1 -> x0, blocking collectives: 66.2 us -> none  [body(): energy_all, phase_all = lax.psum((energy_all, phase_all), ('grp', 'chol'))]
    reduce_sum x160 -> x0, local copies, waits for them, and re-layouts: 16.8 us -> none  [the longest x96 10.9 us: square_trace(): jnp.sum(square * identity_wide, axis=(3, 4))]
    all_gather x2 -> x0, blocking collectives: 15.4 us -> none  [the longest x1 8.62 us: body(): lax.all_gather(green, 'grp', axis=2, tiled=True)]
    reshape x7 -> x3, local copies, waits for them, and re-layouts: 15.5 us -> 2.13 us  [the longest x1 0.8 us: body(): total[:, :, :4].reshape(2, 2, WG, 4)]
  transfers between devices with their start and end apart: 2 -> 0, of which waited for: 2 -> 0; matrix products, arithmetic and copies ran while one was open for 25% -> 0% of each run, Pallas kernels for 0% -> 0%
where the time goes in v1:
time: 125 us; the launch traced here: 124 us
  Pallas kernels  108 us (86%)
  local copies, waits for them, and re-layouts  9.8 us (8%)
  other arithmetic  4.86 us (4%)
    pallas_call x1, Pallas kernels, contract(): pl.pallas_call(contract_kernel, out_shape=(jax.ShapeDtypeStruct((16, 2 *...  54.8 us
    pallas_call x1, Pallas kernels, gather(): pl.pallas_call(gather_kernel, out_shape=(shape((WG, 4, 4, 4) + shard.shap...  35 us
    pallas_call x1, Pallas kernels, reduce_all(): pl.pallas_call(reduce_kernel, out_shape=(jax.ShapeDtypeStruct((2, 8, 128)...  18 us

profile of v1, /device:TPU:1, one launch (start us, length us, event | category | flops | bytes accessed | tf_op | source)
XLA Modules:
  0.0 124.3 jit_solution(1762285687605481616)
XLA Ops:
  0.6 0.0 copy-start
  0.6 0.8 copy.48
  1.4 0.7 reshape.144.ids_a
  2.1 0.9 copy.49
  3.0 0.7 reshape.145.shard
  3.6 0.6 reshape_reshape.3.ids
  4.3 0.7 convert_element_type.40
  5.0 0.7 convert_bitcast_fusion
  5.6 0.1 copy.52
  5.7 0.7 copy.51
  6.5 0.7 select_maximum_fusion.meta
  7.1 35.0 %gather_green.1 = (bf16[4,4,4,4,32,256]{5,4,3,2,1,0:T(8,128)(2,1)}, bf16[64,128,128]{2,1,0:T(8,128)(2,1)}, s32[1,128]{1,0:T(1,128)}, f32[16,64]{1,0:T(8,128)}, f...) custom-call(bf16[4,32,256]{2,1,0:T(8,128)(2,1)} %reshape.145.shard, bf16[64,128,128]{2,1,0:T(8,128)(2,1)} %vec_a.1, ...), custom_call_target="tpu_custom_call" | custom-call | tf_op jit(solution)/shard_map/gather_green/pallas_call | solution.py:141
  42.2 0.0 copy-done
  42.2 0.7 constant_dynamic-slice_fusion.1
  42.9 0.7 pad_maximum_fusion.noise
  43.6 0.0 copy-start.1
  43.6 0.0 copy-start.2
  43.6 54.8 %tee_and_traces.1 = (f32[16,128]{1,0:T(8,128)}, f32[8,128]{1,0:T(8,128)}) custom-call(s32[128]{0:T(128)} %reshape.144.ids_a, s32[128]{0:T(128)} %bitcast.57, bf16[64,128,128]{2,1,0:T(8,128)(2,1)} %vec_a.1, bf16[64,128,128]{2,1,0:T(8,128)(2,1)} %get-tuple-element.16.vec_b, bf16[4,4,4,2,64,256]{5,4,3,2,1,0:T(8,128)(2,1)} %bitcast.41, ...), custom_call_target="tpu_custom_call" | custom-call | tf_op jit(solution)/shard_map/tee_and_traces/pallas_call | solution.py:259
  98.4 18.0 %reduce_terms.1 = (f32[2,8,128]{2,1,0:T(8,128)}, f32[16,128]{1,0:T(8,128)}) custom-call(f32[8,128]{1,0:T(8,128)} %get-tuple-element.20.part, f32[16,128]{1,0:T(8,128)} %get-tuple-element.19.bias), custom_call_target="tpu_custom_call" | custom-call | tf_op jit(solution)/shard_map/reduce_terms/pallas_call | solution.py:332
  116.4 0.8 slice.36
  117.1 0.8 maximum_select_fusion
  117.9 0.6 copy.55
  118.5 0.8 copy.70
  119.4 0.1 slice.39
  119.4 0.6 constant_dynamic-slice_fusion
  120.1 0.1 slice_exponential_fusion
  120.1 0.1 max.17
  120.2 0.1 exp.17
  120.3 0.0 copy-done.1
  120.3 0.1 slice_convert_fusion
  120.4 0.1 copy.75
  120.5 0.6 dynamic_slice.16
  121.1 0.1 slice_convert_fusion.1
  121.1 0.1 eq.38
  121.2 0.1 copy.77
  121.3 0.1 iota_compare_fusion.1
  121.4 0.1 lt.44
  121.5 0.1 fusion.4
  121.6 0.1 reduce_window_sum.11
  121.7 0.2 fusion.5
  121.9 0.1 eq.42
  122.0 0.1 copy.62
  122.1 0.1 gt.15
  122.2 0.1 copy.63
  122.3 0.1 convert_reduce_fusion
  122.3 0.1 max.18
  122.4 0.1 exp.18
  122.5 0.6 multiply_reduce_fusion
  123.2 0.1 convert_element_type.46
  123.2 0.0 copy-done.2
  123.3 1.1 fusion.1
  (10 shorter events, 0.1 us)
Async XLA Ops:
  0.6 41.6 %copy-start = (f32[16,64]{1,0:T(8,128)S(1)}, f32[16,64]{1,0:T(8,128)}, u32[]{:S(2)}) copy-start(f32[16,64]{1,0:T(8,128)} %noise.1) | copy-start | bytes 12292
  43.6 76.7 %copy-start.1 = (f32[4,8,128]{2,1,0:T(8,128)S(1)}, f32[4,8,128]{2,1,0:T(8,128)}, u32[]{:S(2)}) copy-start(f32[4,8,128]{2,1,0:T(8,128)} %get-tuple-element.23) | copy-start | bytes 49156
  43.6 79.7 %copy-start.2 = (bf16[4,32,2,4,128]{4,3,2,1,0:T(4,128)(2,1)S(1)}, bf16[4,32,2,4,128]{4,3,2,1,0:T(4,128)(2,1)}, u32[]{:S(2)}) copy-start(bf16[4,32,2,4,128]{4,3,2,1,0:T(4,128)(2,1)} %get-tuple-element.24) | copy-start | bytes 786436

commit v2 on v1

v2 whole, which is shorter than its diff:
```python
import functools
import math

import jax
import jax.numpy as jnp
from jax import lax
from jax.experimental import pallas as pl
from jax.experimental.pallas import tpu as pltpu
from jax.sharding import PartitionSpec as P

MESH = pl.DeviceIdType.MESH
BF16 = jnp.bfloat16
F32 = jnp.float32
KMAX = 4
GROUPS = 4
WG = 4
ROOT = math.sqrt(0.005)
MB = 2**20

def position():
    grp = lax.axis_index("grp")
    chol = lax.axis_index("chol")
    x = (grp // 2) * 2 + (chol // 4) % 2
    return x, chol // 8, chol % 4, grp % 2


def device(x, y, z, core):
    return ((x // 2) * 2 + core, y * 8 + (x % 2) * 4 + z)


STREAMS = (
    (0, (0, 16), (0, 256), "xyz"),
    (0, (16, 16), (0, 128), "yzx"),
    (0, (16, 16), (128, 128), "zxy"),
    (1, (0, 32), (0, 256), "yzx"),
    (2, (0, 32), (0, 256), "zxy"),
    (3, (0, 32), (0, 256), "xyz"),
)
STEP = 16


def diagonal(block, masks, keep):
    merged = block[0:16]
    for r in range(1, 8):
        merged = jnp.where(masks[r], block[16 * r : 16 * r + 16], merged)
    return jnp.sum(jnp.where(keep, merged, jnp.zeros_like(merged)).astype(F32), axis=0, keepdims=True)


def fused_kernel(
    shard, vectors, ids, noise, meta, green,
    total_ref, bias_ref, bias2_ref, meta_all, green_all,
    g0, g1, g2, g3, vec, ids_v, ids_s, noise2, acc, diag, part, slots, slots2, own2,
    local_sem, send_sem, recv_sem, pair_send, pair_recv, group_send, group_recv,
    send1, recv1, send2, recv2,
):
    chunks = (g0, g1, g2, g3)
    x, y, z, core = position()
    grp = lax.axis_index("grp")
    count = vectors.shape[0]
    here = {"x": x, "y": y, "z": z}
    sibling = device(x, y, z, 1 - core)
    across = [device((x + 2) % 4, y, z, core), device((x + 2) % 4, y, z, 1 - core)]
    plane = [
        device((x + i) % 4, (y + j) % 4, z, core)
        for i in range(4) for j in range(4) if i + j > 0
    ]
    column = [
        device(x, y, (z + i) % 4, (core + k) % 2)
        for k in range(2) for i in range(4) if i + k > 0
    ]
    everyone = plane + column + [across[1]]
    barrier = pltpu.get_barrier_semaphore()
    for target in everyone:
        pl.semaphore_signal(barrier, inc=1, device_id=target, device_id_type=MESH)

    local = [
        pltpu.make_async_copy(vectors, vec.at[pl.ds(0, count)], local_sem.at[0]),
        pltpu.make_async_copy(ids, ids_s.at[pl.ds(0, count)], local_sem.at[1]),
        pltpu.make_async_copy(meta, meta_all.at[grp], local_sem.at[2]),
        pltpu.make_async_copy(green, green_all.at[grp], local_sem.at[3]),
    ]
    for copy in local:
        copy.start()
    for c in range(4):
        chunks[c][x, y, z] = shard[c]
    acc[...] = jnp.zeros_like(acc)
    pl.semaphore_wait(barrier, len(everyone))

    def remote(source, target, send, recv, where):
        return pltpu.make_async_remote_copy(
            src_ref=source, dst_ref=target, send_sem=send, recv_sem=recv,
            device_id=where, device_id_type=MESH,
        )

    def move(stream, phase, kind):
        chunk, rows, cols, order = STREAMS[stream]
        axis, free = order[phase], order[:phase]
        up, down, far = dict(here), dict(here), dict(here)
        up[axis] = (here[axis] + 1) % 4
        down[axis] = (here[axis] + 3) % 4
        far[axis] = (here[axis] + 2) % 4
        at, to, span = here, (up, down, far)[kind % 3], slice(None)
        if phase == 2 and kind == 2:
            at, to, span = down, up, pl.ds(0, 2)
        if phase == 2 and kind == 3:
            at, to, span = up, down, pl.ds(2, 2)
        index = [(span if a == order[0] else slice(None)) if a in free else at[a] for a in "xyz"]
        ref = chunks[chunk].at[(*index, pl.ds(*rows), pl.ds(*cols))]
        return remote(
            ref, ref, send_sem.at[stream, phase, kind], recv_sem.at[stream, phase, kind],
            device(to["x"], to["y"], to["z"], core),
        )

    def begin(stream, phase):
        for kind in (0, 1) if phase == 2 else (0, 1, 2):
            move(stream, phase, kind).start()

    def arrive(stream, phase):
        for kind in range(3):
            move(stream, phase, kind).wait_recv()

    def forward(stream):
        move(stream, 2, 0).wait_recv()
        move(stream, 2, 2).start()
        move(stream, 2, 1).wait_recv()
        move(stream, 2, 3).start()

    def finish(stream):
        move(stream, 2, 2).wait_recv()
        move(stream, 2, 3).wait_recv()
        for phase in range(3):
            for kind in range(4 if phase == 2 else 3):
                move(stream, phase, kind).wait_send()

    swaps = [
        remote(ids, ids_v, pair_send.at[0], pair_recv.at[0], sibling),
        remote(noise, noise2, pair_send.at[1], pair_recv.at[1], sibling),
        remote(vectors, vec.at[pl.ds(count, count)], pair_send.at[2], pair_recv.at[2], sibling),
    ]
    groups = []
    for i, target in enumerate([sibling] + across):
        groups.append(remote(meta, meta_all.at[grp], group_send.at[0, i], group_recv.at[0, i], target))
        groups.append(remote(green, green_all.at[grp], group_send.at[1, i], group_recv.at[1, i], target))

    first = (0, 1, 2)
    for s in first:
        begin(s, 0)
    for copy in swaps:
        copy.start()
    for phase in (1, 2):
        for s in first:
            arrive(s, phase - 1)
            begin(s, phase)
    for s in (3, 4, 5):
        begin(s, 0)
    for s in first:
        forward(s)
    for copy in groups:
        copy.start()
    swaps[0].wait()
    ids_copy = pltpu.make_async_copy(ids_v, ids_s.at[pl.ds(count, count)], local_sem.at[4])
    ids_copy.start()
    for copy in local:
        copy.wait()
    ids_copy.wait()
    for s in first:
        finish(s)

    def advance(streams, phase):
        def run():
            for s in streams:
                arrive(s, phase - 1)
                begin(s, phase)
        return run

    def onward(streams):
        def run():
            for s in streams:
                forward(s)
        return run

    events = {
        0: advance((3,), 1),
        1: advance((4, 5), 1),
        2: advance((3,), 2),
        3: advance((4, 5), 2),
        4: lambda: swaps[2].wait(),
        6: onward((3,)),
        7: onward((4, 5)),
    }

    lane16 = lax.broadcasted_iota(jnp.int32, (16, 128), 1)
    masks = [(lane16 // 16) == r for r in range(8)]
    keep = (lane16 % 16) == lax.broadcasted_iota(jnp.int32, (16, 128), 0)

    def compute(chunk, actions):
        ref = chunks[chunk]

        def step(turn, carry):
            for when, action in actions.items():
                pl.when(turn == when)(action)
            places = []
            for k in range(STEP):
                g = turn * STEP + k
                for j in range(2):
                    b = ids_s[g, j]
                    places.append((lax.rem(lax.div(b, 2), 2), lax.div(b, 4), lax.rem(b, 2) * 2))
            for xh in range(2):
                w = xh * 4 + chunk
                lefts, rights = [], []
                for k in range(STEP):
                    g = turn * STEP + k
                    rows = [
                        ref[xh * 2 + px, py, pl.ds(pz, 2)].reshape(64, 256)
                        for px, py, pz in places[2 * k : 2 * k + 2]
                    ]
                    tee = jnp.dot(
                        vec[g], jnp.concatenate(rows, 0), preferred_element_type=F32
                    ).astype(BF16)
                    real, imag = tee[:, :128], tee[:, 128:]
                    diag[w, pl.ds(g, 1)] = diagonal(real, masks, keep)
                    diag[8 + w, pl.ds(g, 1)] = diagonal(imag, masks, keep)
                    lefts.append(tee)
                    rights += [tee, jnp.concatenate([-imag, real], 1)]
                acc[w] += jnp.dot(
                    jnp.concatenate(lefts, 1), jnp.concatenate(rights, 0), preferred_element_type=F32
                )
            return carry

        lax.fori_loop(0, 2 * count // STEP, step, 0)

    compute(0, events)
    for chunk in (1, 2, 3):
        finish(chunk + 2)
        compute(chunk, {})

    row16 = lax.broadcasted_iota(jnp.int32, (16, 128), 0)
    bias = jnp.zeros((16, 2 * count), F32)
    for r in range(16):
        bias += lax.dot_general(
            (row16 == r).astype(BF16), diag[r].astype(BF16),
            (((1,), (1,)), ((), ())), preferred_element_type=F32,
        )
    bias = 2.0 * bias
    bias_ref[...] = bias
    eye = lax.broadcasted_iota(jnp.int32, (128, 128), 0) == lax.broadcasted_iota(jnp.int32, (128, 128), 1)
    row8 = lax.broadcasted_iota(jnp.int32, (8, 128), 0)
    kx = [jnp.zeros((8, 128), F32), jnp.zeros((8, 128), F32)]
    for w in range(8):
        for c in range(2):
            line = jnp.sum(
                jnp.where(eye, acc[w, :, c * 128 : (c + 1) * 128], 0.0), axis=0, keepdims=True
            )
            kx[c] += jnp.where(row8 == w, line, 0.0)
    swaps[1].wait()

    def fields_of(ref):
        return jnp.concatenate(
            [jnp.where(core == 0, ref[0:4], ref[4:8]), jnp.where(core == 0, ref[8:12], ref[12:16])], 0
        )

    fields = jnp.concatenate([fields_of(noise), fields_of(noise2)], 1)
    re, im = bias[:8], bias[8:]
    energy_re = 0.5 * (re * re - im * im) - kx[0]
    energy_im = re * im - kx[1]
    shift_re, shift_im = -ROOT * re, -ROOT * im
    phase_re = fields * shift_re - 0.5 * (shift_re * shift_re - shift_im * shift_im)
    phase_im = fields * shift_im - shift_re * shift_im
    lane8 = lax.broadcasted_iota(jnp.int32, (8, 128), 1)
    result = jnp.zeros((8, 128), F32)
    for i, value in enumerate((energy_re, energy_im, phase_re, phase_im)):
        result = jnp.where(lane8 == i, jnp.sum(value, axis=1, keepdims=True), result)
    part[...] = result

    me = x * 4 + y
    me2 = core * 4 + z
    slots[me] = result
    round1 = [
        remote(part, slots.at[me], send1.at[i], recv1.at[i], target)
        for i, target in enumerate(plane)
    ]
    for copy in round1:
        copy.start()
    swap = remote(bias_ref, bias2_ref, pair_send.at[3], pair_recv.at[3], sibling)
    swap.start()
    for copy in groups:
        copy.wait()
    for copy in round1:
        copy.wait()
    mine = jnp.sum(slots[...], axis=0)
    own2[...] = mine
    slots2[me2] = mine
    round2 = [
        remote(own2, slots2.at[me2], send2.at[i], recv2.at[i], target)
        for i, target in enumerate(column)
    ]
    for copy in round2:
        copy.start()
    for copy in round2:
        copy.wait()
    total_ref[0] = jnp.sum(slots2[0:4], axis=0)
    total_ref[1] = jnp.sum(slots2[4:8], axis=0)
    swap.wait()


def fused(shard, vectors, ids, noise, meta, green):
    vmem = pl.BlockSpec(memory_space=pltpu.VMEM)
    hbm = pl.BlockSpec(memory_space=pl.ANY)
    shape = jax.ShapeDtypeStruct
    count = vectors.shape[0]
    dma = pltpu.SemaphoreType.DMA
    streams = len(STREAMS)
    return pl.pallas_call(
        fused_kernel,
        out_shape=(
            shape((2, 8, 128), F32),
            shape((16, 2 * count), F32),
            shape((16, 2 * count), F32),
            shape((GROUPS,) + meta.shape, meta.dtype),
            shape((GROUPS,) + green.shape, green.dtype),
        ),
        in_specs=[vmem, hbm, vmem, vmem, vmem, hbm],
        out_specs=(vmem, vmem, vmem, vmem, hbm),
        scratch_shapes=[pltpu.VMEM((4, 4, 4) + shard.shape[1:], BF16)] * 4
        + [
            pltpu.VMEM((2 * count,) + vectors.shape[1:], BF16),
            pltpu.VMEM(ids.shape, ids.dtype),
            pltpu.SMEM((2 * count, 2), ids.dtype),
            pltpu.VMEM(noise.shape, F32),
            pltpu.VMEM((8, 128, 256), F32),
            pltpu.VMEM((16, 2 * count, 128), F32),
            pltpu.VMEM((8, 128), F32),
            pltpu.VMEM((16, 8, 128), F32),
            pltpu.VMEM((8, 8, 128), F32),
            pltpu.VMEM((8, 128), F32),
            dma((5,)), dma((streams, 3, 4)), dma((streams, 3, 4)),
            dma((4,)), dma((4,)), dma((2, 3)), dma((2, 3)),
            dma((15,)), dma((15,)), dma((7,)), dma((7,)),
        ],
        compiler_params=pltpu.CompilerParams(
            collective_id=0, has_side_effects=True, vmem_limit_bytes=48 * MB
        ),
        name="fused_step",
    )(shard, vectors, ids, noise, meta, green)


def body(green, chol_blocks, block_ids, noise, weights, copies, owners):
    grp = lax.axis_index("grp")
    core = grp % 2
    rows, _, _, electrons = green.shape
    vectors = chol_blocks.shape[0]
    shard = jnp.transpose(green, (2, 0, 1, 3)).reshape(WG, rows, 2 * electrons)
    meta = jnp.concatenate(
        [weights[:, None], copies[:, None].astype(F32), owners.astype(F32)], axis=1
    )
    meta = jnp.pad(meta, ((0, 4), (0, 128 - 6)))
    total, bias, bias2, meta_all, green_all = fused(
        shard, chol_blocks, block_ids, noise, meta, green
    )
    meta_all = meta_all[:, :WG].reshape(GROUPS * WG, -1)
    all_weights = meta_all[:, 0]
    all_copies = meta_all[:, 1].astype(jnp.int32)
    all_owners = meta_all[:, 2:6].astype(jnp.int32)
    kept = jnp.arange(KMAX, dtype=jnp.int32)[None, :] < all_copies[:, None]
    targets = jnp.arange(GROUPS, dtype=jnp.int32)
    hits = ((all_owners[:, :, None] == targets[None, None, :]) & kept[:, :, None]).astype(jnp.int32)
    hits = hits.reshape(GROUPS * WG * KMAX, GROUPS)
    ranks = jnp.cumsum(hits, axis=0, dtype=jnp.int32) - hits
    slots = jnp.sum(hits * (ranks + targets[None, :] * WG), axis=1, dtype=jnp.int32)
    live = jnp.sum(hits, axis=1, dtype=jnp.int32) > 0
    own_slots = grp * WG + jnp.arange(WG, dtype=jnp.int32)
    route = ((slots[:, None] == own_slots[None, :]) & live[:, None]).astype(F32)
    route = jnp.sum(route.reshape(GROUPS * WG, KMAX, WG), axis=1)
    moved_green = jnp.einsum(
        "gmcwn,gws->mcsn", green_all, route.reshape(GROUPS, WG, WG).astype(BF16),
        preferred_element_type=F32,
    ).astype(BF16)

    terms = jnp.transpose(total[:, :, :4].reshape(2, 2, WG, 4), (3, 1, 0, 2)).reshape(4, GROUPS * WG)
    every_weight = all_weights * jnp.exp(terms[2]) * jnp.maximum(jnp.cos(terms[3]), 0.0)
    energy = lax.dynamic_slice_in_dim(terms[:2], grp * WG, WG, axis=1)
    new_weights = lax.dynamic_slice_in_dim(every_weight, grp * WG, WG, axis=0)
    moved_weights = jnp.sum(route * every_weight[:, None], axis=0)
    ours = bias[:, :vectors].reshape(2, 2, WG, vectors)
    theirs = bias2[:, vectors:].reshape(2, 2, WG, vectors)
    force_bias = jnp.where(
        core == 0, jnp.stack([ours, theirs], axis=2), jnp.stack([theirs, ours], axis=2)
    ).reshape(2, GROUPS * WG, vectors)
    return (force_bias, energy, new_weights, moved_green, moved_weights)


def solution(mesh):
    return jax.shard_map(
        body,
        mesh=mesh,
        in_specs=(
            P("chol", None, "grp", None),
            P(("grp", "chol"), None, None),
            P(("grp", "chol"), None),
            P(None, ("grp", "chol")),
            P("grp"),
            P("grp"),
            P("grp", None),
        ),
        out_specs=(
            P(None, None, ("grp", "chol")),
            P(None, "grp"),
            P("grp"),
            P("chol", None, "grp", None),
            P("grp"),
        ),
        check_vma=False,
    )
```

time: 125 us -> 101 us (0.81)
  Pallas kernels: 108 us -> 87 us
  other arithmetic: 4.86 us -> 2.83 us
    pallas_call x3 -> x1, Pallas kernels: 108 us -> 87 us  [fused(): pl.pallas_call(fused_kernel, out_shape=(shape((2, 8, 128), F32), shape((1...]
    unnamed x9, local copies, waits for them, and re-layouts: 0.95 us -> 4.06 us
where the time goes in v2:
time: 101 us
  Pallas kernels  87 us (86%)
  local copies, waits for them, and re-layouts  8.92 us (9%)
  other arithmetic  2.83 us (3%)
  matrix products  1.06 us (1%)
    pallas_call x1, Pallas kernels, fused(): pl.pallas_call(fused_kernel, out_shape=(shape((2, 8, 128), F32), shape((1...  87 us
    unnamed x9, local copies, waits for them, and re-layouts  4.06 us

profile of v2, /device:TPU:1, one launch (start us, length us, event | category | flops | bytes accessed | tf_op | source)
XLA Modules:
  0.0 100.6 jit_solution(2371009102742141975)
XLA Ops:
  0.6 0.9 copy.42
  1.6 0.8 copy.45.ids
  2.4 0.7 convert_element_type.40
  3.0 0.7 convert_bitcast_fusion
  3.7 0.1 copy.44
  3.8 0.7 copy.43
  4.5 0.1 select_maximum_fusion.meta
  4.6 0.0 copy-start
  4.6 1.6 %copy-done = bf16[64,128,128]{2,1,0:T(8,128)(2,1)S(1)} copy-done((bf16[64,128,128]{2,1,0:T(8,128)(2,1)S(1)}, bf16[64,128,128]{2,1,0:T(8,128)(2,1)}, u32[]{:S(2)}) %copy-start) | copy-done | bytes 2097176
  6.2 0.0 copy-start.1
  6.2 0.8 copy-done.1
  7.0 0.0 copy-start.2
  7.0 0.7 copy-done.2
  7.7 87.0 %fused_step.1 = (f32[2,8,128]{2,1,0:T(8,128)S(1)}, f32[16,128]{1,0:T(8,128)S(1)}, f32[16,128]{1,0:T(8,128)S(1)}, f32[4,8,128]{2,1,0:T(8,128)S(1)}, bf16[4,32,2,4,128]{4,3,2,1,0:T(4,128)(2,1)S(1)}) custom-call(bf16[4,32,256]{2,1,0:T(8,128)(2,1)S(1)} %reshape.121.shard, bf16[64,128,128]{2,1,0:T(8,128)(2,1)S(1)} %copy-done, s32[64,2]{1,0:T(8,128)S(1)} %copy.45.ids, ...), custom_call_target="tpu_custom_call" | custom-call | tf_op jit(solution)/shard_map/fused_step/pallas_call | solution.py:313
  94.8 0.1 slice.36
  94.9 0.6 copy.46
  95.5 0.1 copy.61
  95.6 0.1 slice.39
  95.7 0.6 constant_dynamic-slice_fusion
  96.3 0.1 slice_exponential_fusion
  96.4 0.1 max.17
  96.5 0.1 exp.17
  96.6 0.1 slice_convert_fusion
  96.6 0.1 copy.64
  96.7 0.6 dynamic_slice.7
  97.3 0.1 slice_convert_fusion.1
  97.4 0.1 eq.38
  97.5 0.1 copy.66
  97.6 0.1 iota_compare_fusion.1
  97.6 0.1 lt.38
  97.8 0.1 fusion.4
  97.8 0.1 reduce_window_sum.11
  97.9 0.2 fusion.5
  98.1 0.1 eq.42
  98.2 0.1 copy.53
  98.3 0.1 gt.15
  98.4 0.1 copy.54
  98.5 0.1 convert_reduce_fusion
  98.6 0.1 max.18
  98.7 0.1 exp.18
  98.8 0.6 multiply_reduce_fusion
  99.4 0.1 convert_element_type.46
  99.5 1.1 %fusion.1 = bf16[32,2,4,128]{3,2,1,0:T(4,128)(2,1)} fusion(bf16[4,32,2,4,128]{4,3,2,1,0:T(4,128)(2,1)S(1)} %get-tuple-element.14, bf16[4,4,4,1,1]{1,0,2,4,3:T(4,128)(2,1)S(1)} %bitcast.40), kind=kOutput, calls=%fused_computation.2 | convolution fusion | flops 1081344 | bytes 327808 | tf_op jit(solution)/shard_map/gmcwn,gws->mcsn/dot_general | solution.py:374
  (12 shorter events, 0.1 us)
Async XLA Ops:
  4.6 1.6 %copy-start = (bf16[64,128,128]{2,1,0:T(8,128)(2,1)S(1)}, bf16[64,128,128]{2,1,0:T(8,128)(2,1)}, u32[]{:S(2)}) copy-start(bf16[64,128,128]{2,1,0:T(8,128)(2,1)} %vectors.1) | copy-start | bytes 6291460
  6.2 0.8 copy-start.1
  7.0 0.7 copy-start.2

commit v3 on v2

v3 whole, which is shorter than its diff:
```python
import functools
import math

import jax
import jax.numpy as jnp
from jax import lax
from jax.experimental import pallas as pl
from jax.experimental.pallas import tpu as pltpu
from jax.sharding import PartitionSpec as P

MESH = pl.DeviceIdType.MESH
BF16 = jnp.bfloat16
F32 = jnp.float32
KMAX = 4
GROUPS = 4
WG = 4
ROOT = math.sqrt(0.005)
MB = 2**20

def position():
    grp = lax.axis_index("grp")
    chol = lax.axis_index("chol")
    x = (grp // 2) * 2 + (chol // 4) % 2
    return x, chol // 8, chol % 4, grp % 2


def device(x, y, z, core):
    return ((x // 2) * 2 + core, y * 8 + (x % 2) * 4 + z)


WINDOWS = (((0, 16), (0, 256)), ((16, 16), (0, 128)), ((16, 16), (128, 128)))
ORDERS = ("xyz", "yzx", "zxy")
STREAMS = tuple(
    (chunk, *WINDOWS[i], ORDERS[(chunk + i) % 3]) for chunk in range(4) for i in range(3)
)
STEP = 32


def diagonal(block, masks, keep):
    merged = block[0:16]
    for r in range(1, 8):
        merged = jnp.where(masks[r], block[16 * r : 16 * r + 16], merged)
    return jnp.sum(jnp.where(keep, merged, jnp.zeros_like(merged)).astype(F32), axis=0, keepdims=True)


def fused_kernel(
    shard, vectors, ids, noise, weights, copies, owners,
    force_ref, energy_ref, new_ref, moved_ref, green_ref,
    g0, g1, g2, g3, vec, ids_v, ids_s, noise1, noise2, acc, diag, part, slots, slots2, own2,
    bias1, bias2, shards, w_all, c_all, o_all, w_s, c_s, o_s,
    local_sem, send_sem, recv_sem, pair_send, pair_recv, group_send, group_recv,
    send1, recv1, send2, recv2,
):
    chunks = (g0, g1, g2, g3)
    x, y, z, core = position()
    grp = lax.axis_index("grp")
    count = vectors.shape[0]
    here = {"x": x, "y": y, "z": z}
    sibling = device(x, y, z, 1 - core)
    across = [device((x + 2) % 4, y, z, core), device((x + 2) % 4, y, z, 1 - core)]
    plane = [
        device((x + i) % 4, (y + j) % 4, z, core)
        for i in range(4) for j in range(4) if i + j > 0
    ]
    column = [
        device(x, y, (z + i) % 4, (core + k) % 2)
        for k in range(2) for i in range(4) if i + k > 0
    ]
    everyone = plane + column + [across[1]]
    barrier = pltpu.get_barrier_semaphore()
    for target in everyone:
        pl.semaphore_signal(barrier, inc=1, device_id=target, device_id_type=MESH)

    starts = [
        pltpu.make_async_copy(shard.at[c], chunks[c].at[x, y, z], local_sem.at[c]) for c in range(4)
    ]
    local = [
        pltpu.make_async_copy(vectors, vec.at[pl.ds(0, count)], local_sem.at[4]),
        pltpu.make_async_copy(ids, ids_s.at[0], local_sem.at[5]),
        pltpu.make_async_copy(noise, noise1, local_sem.at[6]),
    ]
    tables = [
        (shard, shards.at[pl.ds(grp * WG, WG)]),
        (weights, w_all.at[grp]),
        (copies, c_all.at[grp]),
        (owners, o_all.at[grp]),
    ]
    local += [
        pltpu.make_async_copy(source, place, local_sem.at[7 + i]) for i, (source, place) in enumerate(tables)
    ]
    for copy in starts + local:
        copy.start()
    acc[...] = jnp.zeros_like(acc)
    for copy in starts:
        copy.wait()
    pl.semaphore_wait(barrier, len(everyone))

    def remote(source, target, send, recv, where):
        return pltpu.make_async_remote_copy(
            src_ref=source, dst_ref=target, send_sem=send, recv_sem=recv,
            device_id=where, device_id_type=MESH,
        )

    def move(stream, phase, kind):
        chunk, rows, cols, order = STREAMS[stream]
        axis, free = order[phase], order[:phase]
        up, down, far = dict(here), dict(here), dict(here)
        up[axis] = (here[axis] + 1) % 4
        down[axis] = (here[axis] + 3) % 4
        far[axis] = (here[axis] + 2) % 4
        at, to, span = here, (up, down, far)[kind % 3], slice(None)
        if phase == 2 and kind == 2:
            at, to, span = down, up, pl.ds(0, 2)
        if phase == 2 and kind == 3:
            at, to, span = up, down, pl.ds(2, 2)
        index = [(span if a == order[0] else slice(None)) if a in free else at[a] for a in "xyz"]
        ref = chunks[chunk].at[(*index, pl.ds(*rows), pl.ds(*cols))]
        return remote(
            ref, ref, send_sem.at[stream, phase, kind], recv_sem.at[stream, phase, kind],
            device(to["x"], to["y"], to["z"], core),
        )

    def begin(stream, phase):
        for kind in (0, 1) if phase == 2 else (0, 1, 2):
            move(stream, phase, kind).start()

    def arrive(stream, phase):
        for kind in range(3):
            move(stream, phase, kind).wait_recv()

    def forward(stream):
        move(stream, 2, 0).wait_recv()
        move(stream, 2, 2).start()
        move(stream, 2, 1).wait_recv()
        move(stream, 2, 3).start()

    def finish(stream):
        move(stream, 2, 2).wait_recv()
        move(stream, 2, 3).wait_recv()
        for phase in range(3):
            for kind in range(4 if phase == 2 else 3):
                move(stream, phase, kind).wait_send()

    swaps = [
        remote(ids, ids_v, pair_send.at[0], pair_recv.at[0], sibling),
        remote(noise, noise2, pair_send.at[1], pair_recv.at[1], sibling),
        remote(vectors, vec.at[pl.ds(count, count)], pair_send.at[2], pair_recv.at[2], sibling),
    ]
    groups = []
    for i, target in enumerate([sibling] + across):
        for j, (source, place) in enumerate(tables):
            groups.append(remote(source, place, group_send.at[j, i], group_recv.at[j, i], target))

    def streams(chunk):
        return range(3 * chunk, 3 * chunk + 3)

    def advance(chunk, phase):
        def run():
            for s in streams(chunk):
                arrive(s, phase - 1)
                begin(s, phase)
        return run

    def onward(chunk):
        def run():
            for s in streams(chunk):
                forward(s)
        return run

    def complete(chunk):
        for s in streams(chunk):
            finish(s)

    for s in streams(0):
        begin(s, 0)
    for copy in swaps:
        copy.start()
    advance(0, 1)()
    advance(0, 2)()
    for s in streams(1):
        begin(s, 0)
    onward(0)()
    swaps[0].wait()
    ids_copy = pltpu.make_async_copy(ids_v, ids_s.at[1], local_sem.at[11])
    ids_copy.start()
    for copy in local:
        copy.wait()
    ids_copy.wait()
    complete(0)

    lane16 = lax.broadcasted_iota(jnp.int32, (16, 128), 1)
    masks = [(lane16 // 16) == r for r in range(8)]
    keep = (lane16 % 16) == lax.broadcasted_iota(jnp.int32, (16, 128), 0)

    def compute(chunk, actions):
        ref = chunks[chunk]

        def step(turn, carry):
            for when, action in actions.items():
                pl.when(turn == when)(action)
            places = []
            part_of = lax.div(turn, count // STEP)
            for k in range(STEP):
                for j in range(2):
                    b = ids_s[part_of, j, lax.rem(turn, count // STEP) * STEP + k]
                    places.append((lax.rem(lax.div(b, 2), 2), lax.div(b, 4), lax.rem(b, 2) * 2))
            for xh in range(2):
                w = xh * 4 + chunk
                lefts, rights = [], []
                for k in range(STEP):
                    g = turn * STEP + k
                    rows = [
                        ref[xh * 2 + px, py, pl.ds(pz, 2)].reshape(64, 256)
                        for px, py, pz in places[2 * k : 2 * k + 2]
                    ]
                    tee = jnp.dot(
                        vec[g], jnp.concatenate(rows, 0), preferred_element_type=F32
                    ).astype(BF16)
                    real, imag = tee[:, :128], tee[:, 128:]
                    diag[w, pl.ds(g, 1)] = diagonal(real, masks, keep)
                    diag[8 + w, pl.ds(g, 1)] = diagonal(imag, masks, keep)
                    lefts.append(tee)
                    rights += [tee, jnp.concatenate([-imag, real], 1)]
                acc[w] += jnp.dot(
                    jnp.concatenate(lefts, 1), jnp.concatenate(rights, 0), preferred_element_type=F32
                )
            return carry

        lax.fori_loop(0, 2 * count // STEP, step, 0)

    for chunk in range(4):
        actions = {}
        if chunk < 3:
            actions = {0: advance(chunk + 1, 1), 1: advance(chunk + 1, 2), 3: onward(chunk + 1)}
        if chunk == 0:
            actions[2] = lambda: swaps[2].wait()
        if chunk == 1:
            for copy in groups:
                copy.start()
        compute(chunk, actions)
        if chunk < 3:
            if chunk < 2:
                for s in streams(chunk + 2):
                    begin(s, 0)
            complete(chunk + 1)

    row16 = lax.broadcasted_iota(jnp.int32, (16, 128), 0)
    bias = jnp.zeros((16, 2 * count), F32)
    for r in range(16):
        bias += lax.dot_general(
            (row16 == r).astype(BF16), diag[r].astype(BF16),
            (((1,), (1,)), ((), ())), preferred_element_type=F32,
        )
    bias = 2.0 * bias
    bias1[...] = bias
    eye = lax.broadcasted_iota(jnp.int32, (128, 128), 0) == lax.broadcasted_iota(jnp.int32, (128, 128), 1)
    row8 = lax.broadcasted_iota(jnp.int32, (8, 128), 0)
    kx = [jnp.zeros((8, 128), F32), jnp.zeros((8, 128), F32)]
    for w in range(8):
        for c in range(2):
            line = jnp.sum(
                jnp.where(eye, acc[w, :, c * 128 : (c + 1) * 128], 0.0), axis=0, keepdims=True
            )
            kx[c] += jnp.where(row8 == w, line, 0.0)
    swaps[1].wait()

    def fields_of(ref):
        return jnp.concatenate(
            [jnp.where(core == 0, ref[0:4], ref[4:8]), jnp.where(core == 0, ref[8:12], ref[12:16])], 0
        )

    fields = jnp.concatenate([fields_of(noise1), fields_of(noise2)], 1)
    re, im = bias[:8], bias[8:]
    energy_re = 0.5 * (re * re - im * im) - kx[0]
    energy_im = re * im - kx[1]
    shift_re, shift_im = -ROOT * re, -ROOT * im
    phase_re = fields * shift_re - 0.5 * (shift_re * shift_re - shift_im * shift_im)
    phase_im = fields * shift_im - shift_re * shift_im
    lane8 = lax.broadcasted_iota(jnp.int32, (8, 128), 1)
    lane_of = ((row8 // 4) * 2 + core) * 4 + row8 % 4
    result = jnp.zeros((8, 128), F32)
    for i, value in enumerate((energy_re, energy_im, phase_re, phase_im)):
        column_sum = jnp.sum(value, axis=1, keepdims=True)
        line = jnp.sum(jnp.where(lane8 == lane_of, column_sum, 0.0), axis=0, keepdims=True)
        result = jnp.where(row8 == i, line, result)
    part[...] = result

    me = x * 4 + y
    me2 = core * 4 + z
    slots[me] = result
    round1 = [
        remote(part, slots.at[me], send1.at[i], recv1.at[i], target)
        for i, target in enumerate(plane)
    ]
    for copy in round1:
        copy.start()
    swap = remote(bias1, bias2, pair_send.at[3], pair_recv.at[3], sibling)
    swap.start()
    for copy in groups:
        copy.wait()
    scalars = [
        pltpu.make_async_copy(source, place, local_sem.at[12 + i])
        for i, (source, place) in enumerate(((w_all, w_s), (c_all, c_s), (o_all, o_s)))
    ]
    for copy in scalars:
        copy.start()
    for copy in scalars:
        copy.wait()
    lane1 = lax.broadcasted_iota(jnp.int32, (1, 128), 1)
    before = jnp.int32(0)
    sources = [jnp.int32(0)] * WG
    weight_line = jnp.zeros((1, 128), F32)
    for w in range(GROUPS * WG):
        live_copies = c_s[w // WG, 0, w % WG]
        weight_line = jnp.where(lane1 == w, w_s[w // WG, 0, w % WG], weight_line)
        for j in range(KMAX):
            hit = jnp.logical_and(j < live_copies, o_s[w // WG, w % WG, j] == grp)
            for s in range(WG):
                sources[s] = jnp.where(jnp.logical_and(hit, before == s), w, sources[s])
            before = before + jnp.where(hit, 1, 0)
    for s in range(WG):
        green_ref[s] = shards[sources[s]]

    for copy in round1:
        copy.wait()
    mine = jnp.sum(slots[...], axis=0)
    own2[...] = mine
    slots2[me2] = mine
    round2 = [
        remote(own2, slots2.at[me2], send2.at[i], recv2.at[i], target)
        for i, target in enumerate(column)
    ]
    for copy in round2:
        copy.start()
    swap.wait()
    theirs = pltpu.roll(bias2[...], 64, 1)[:, :count]
    ours = bias[:, :count]
    for c in range(2):
        for xh in range(2):
            one = ours[c * 8 + xh * 4 : c * 8 + xh * 4 + 4]
            two = theirs[c * 8 + xh * 4 : c * 8 + xh * 4 + 4]
            force_ref[c, xh * 8 : xh * 8 + 8] = jnp.concatenate(
                [jnp.where(core == 0, one, two), jnp.where(core == 0, two, one)], 0
            )
    for copy in round2:
        copy.wait()
    total = jnp.sum(slots2[...], axis=0)
    new = weight_line * jnp.exp(total[2:3]) * jnp.maximum(jnp.cos(total[3:4]), 0.0)
    moved = jnp.zeros((1, 128), F32)
    for s in range(WG):
        picked = jnp.sum(jnp.where(lane1 == sources[s], new, 0.0), axis=1, keepdims=True)
        moved = jnp.where(lane1 == s, picked, moved)
    shifted = jnp.where(row8 == 2, new, total)
    turn_by = lax.rem(128 - grp * WG, 128)
    shifted = pltpu.roll(shifted, turn_by, 1)
    energy_ref[...] = shifted[0:2, :WG]
    new_ref[...] = shifted[2:3, :WG]
    moved_ref[...] = moved[:, :WG]


def fused(shard, vectors, ids, noise, weights, copies, owners):
    vmem = pl.BlockSpec(memory_space=pltpu.VMEM)
    hbm = pl.BlockSpec(memory_space=pl.ANY)
    shape = jax.ShapeDtypeStruct
    count = vectors.shape[0]
    dma = pltpu.SemaphoreType.DMA
    streams = len(STREAMS)
    I32 = jnp.int32
    return pl.pallas_call(
        fused_kernel,
        out_shape=(
            shape((2, GROUPS * WG, count), F32),
            shape((2, WG), F32),
            shape((1, WG), F32),
            shape((1, WG), F32),
            shape(shard.shape, BF16),
        ),
        in_specs=[hbm] * 7,
        out_specs=(vmem,) * 5,
        scratch_shapes=[pltpu.VMEM((4, 4, 4) + shard.shape[1:], BF16)] * 4
        + [
            pltpu.VMEM((2 * count,) + vectors.shape[1:], BF16),
            pltpu.VMEM(ids.shape, I32),
            pltpu.SMEM((2,) + ids.shape, I32),
            pltpu.VMEM(noise.shape, F32),
            pltpu.VMEM(noise.shape, F32),
            pltpu.VMEM((8, 128, 256), F32),
            pltpu.VMEM((16, 2 * count, 128), F32),
            pltpu.VMEM((8, 128), F32),
            pltpu.VMEM((16, 8, 128), F32),
            pltpu.VMEM((8, 8, 128), F32),
            pltpu.VMEM((8, 128), F32),
            pltpu.VMEM((16, 2 * count), F32),
            pltpu.VMEM((16, 2 * count), F32),
            pltpu.VMEM((GROUPS * WG,) + shard.shape[1:], BF16),
            pltpu.VMEM((GROUPS, 1, WG), F32),
            pltpu.VMEM((GROUPS, 1, WG), I32),
            pltpu.VMEM((GROUPS, WG, KMAX), I32),
            pltpu.SMEM((GROUPS, 1, WG), F32),
            pltpu.SMEM((GROUPS, 1, WG), I32),
            pltpu.SMEM((GROUPS, WG, KMAX), I32),
            dma((15,)), dma((streams, 3, 4)), dma((streams, 3, 4)),
            dma((4,)), dma((4,)), dma((4, 3)), dma((4, 3)),
            dma((15,)), dma((15,)), dma((7,)), dma((7,)),
        ],
        compiler_params=pltpu.CompilerParams(
            collective_id=0, has_side_effects=True, vmem_limit_bytes=63 * MB
        ),
        name="fused_step",
    )(shard, vectors, ids, noise, weights, copies, owners)


def body(green, chol_blocks, block_ids, noise, weights, copies, owners):
    rows, _, _, electrons = green.shape
    shard = jnp.transpose(green, (2, 0, 1, 3)).reshape(WG, rows, 2 * electrons)
    force_bias, energy, new_weights, moved_weights, moved = fused(
        shard, chol_blocks, block_ids.T, noise, weights.reshape(1, WG), copies.reshape(1, WG), owners
    )
    moved_green = jnp.transpose(moved.reshape(WG, rows, 2, electrons), (1, 2, 0, 3))
    return (force_bias, energy, new_weights.reshape(WG), moved_green, moved_weights.reshape(WG))


def solution(mesh):
    return jax.shard_map(
        body,
        mesh=mesh,
        in_specs=(
            P("chol", None, "grp", None),
            P(("grp", "chol"), None, None),
            P(("grp", "chol"), None),
            P(None, ("grp", "chol")),
            P("grp"),
            P("grp"),
            P("grp", None),
        ),
        out_specs=(
            P(None, None, ("grp", "chol")),
            P(None, "grp"),
            P("grp"),
            P("chol", None, "grp", None),
            P("grp"),
        ),
        check_vma=False,
    )
```

time: 101 us -> 101 us (level)
  Pallas kernels: 87 us -> 91.8 us
  other arithmetic: 2.83 us -> 0 us
  matrix products: 1.06 us -> 0 us
    pallas_call x1, Pallas kernels: 87 us -> 91.8 us  [fused(): pl.pallas_call(fused_kernel, out_shape=(shape((2, GROUPS * WG, count), F3...]
    convert_element_type x5 -> x0, other arithmetic: 1.57 us -> none  [the longest x1 0.68 us: body(): owners.astype(F32)]
    reshape x1 -> x2, local copies, waits for them, and re-layouts: 0.11 us -> 1.54 us  [body(): moved.reshape(WG, rows, 2, electrons)]
    dynamic_slice x2 -> x0, local copies, waits for them, and re-layouts: 1.23 us -> none  [the longest x1 0.64 us: body(): energy = lax.dynamic_slice_in_dim(terms[:2], grp * WG, WG, axis=1)]
    dot_general x1 -> x0, matrix products: 1.06 us -> none  [body(): jnp.einsum('gmcwn,gws->mcsn', green_all, route.reshape(GROUPS, WG, WG).as...]
    unnamed x9 -> x4, local copies, waits for them, and re-layouts: 4.06 us -> 4.85 us
where the time goes in v3:
time: 101 us; the launch traced here: 100 us
  Pallas kernels  91.8 us (91%)
  local copies, waits for them, and re-layouts  7.96 us (8%)
    pallas_call x1, Pallas kernels, fused(): pl.pallas_call(fused_kernel, out_shape=(shape((2, GROUPS * WG, count), F3...  91.8 us
    unnamed x4, local copies, waits for them, and re-layouts  4.85 us

profile of v3, /device:TPU:1, one launch (start us, length us, event | category | flops | bytes accessed | tf_op | source)
XLA Modules:
  0.0 100.4 jit_solution(11854635670612014050)
XLA Ops:
  0.6 0.9 copy.12
  1.5 0.7 reshape.28.shard
  2.2 91.8 %fused_step.1 = (f32[2,16,64]{2,1,0:T(8,128)}, f32[2,4]{1,0:T(2,128)}, f32[1,4]{1,0:T(1,128)}, f32[1,4]{1,0:T(1,128)}, bf16[4,32,256]{2,1,0:T(8,128)(2,1)}) custom-call(bf16[4,32,256]{2,1,0:T(8,128)(2,1)} %reshape.28.shard, bf16[64,128,128]{2,1,0:T(8,128)(2,1)} %vectors.1, s32[2,64]{1,0:T(2,128)} %bitcast.11, f32[16,64]{1,0:T(8,128)} %noise.1, ...), custom_call_target="tpu_custom_call" | custom-call | tf_op jit(solution)/shard_map/fused_step/pallas_call | solution.py:369
  94.0 0.9 reshape.32
  94.9 0.7 copy.15
  95.5 1.3 %copy.20 = f32[2,16,64]{2,1,0:T(8,128)} copy(f32[2,16,64]{2,1,0:T(8,128)} %get-tuple-element.20) | data formatting | bytes 16384
  96.9 1.2 %copy.21 = f32[2,4]{1,0:T(2,128)} copy(f32[2,4]{1,0:T(2,128)} %get-tuple-element.21) | data formatting | bytes 64
  98.1 1.2 %copy.22 = f32[4]{0:T(128)} copy(f32[4]{0:T(128)} %bitcast.15) | data formatting | bytes 32
  99.3 1.1 %copy.23 = f32[4]{0:T(128)} copy(f32[4]{0:T(128)} %bitcast.14) | data formatting | bytes 32

commit v4 on v3

--- a/solution.py
+++ b/solution.py
@@ -38,16 +38,16 @@
 
 def diagonal(block, masks, keep):
     merged = block[0:16]
-    for r in range(1, 8):
+    for r in range(1, 4):
         merged = jnp.where(masks[r], block[16 * r : 16 * r + 16], merged)
     return jnp.sum(jnp.where(keep, merged, jnp.zeros_like(merged)).astype(F32), axis=0, keepdims=True)
 
 
 def fused_kernel(
-    shard, vectors, ids, noise, weights, copies, owners,
+    green, vectors, ids, noise, weights, copies, owners,
     force_ref, energy_ref, new_ref, moved_ref, green_ref,
     g0, g1, g2, g3, vec, ids_v, ids_s, noise1, noise2, acc, diag, part, slots, slots2, own2,
-    bias1, bias2, shards, w_all, c_all, o_all, w_s, c_s, o_s,
+    bias1, bias2, green_v, shards, w_all, c_all, o_all, w_s, c_s, o_s,
     local_sem, send_sem, recv_sem, pair_send, pair_recv, group_send, group_recv,
     send1, recv1, send2, recv2,
 ):
@@ -71,28 +71,34 @@
     for target in everyone:
         pl.semaphore_signal(barrier, inc=1, device_id=target, device_id_type=MESH)
 
-    starts = [
-        pltpu.make_async_copy(shard.at[c], chunks[c].at[x, y, z], local_sem.at[c]) for c in range(4)
-    ]
+    load = pltpu.make_async_copy(green, green_v, local_sem.at[0])
+    load.start()
     local = [
         pltpu.make_async_copy(vectors, vec.at[pl.ds(0, count)], local_sem.at[4]),
         pltpu.make_async_copy(ids, ids_s.at[0], local_sem.at[5]),
         pltpu.make_async_copy(noise, noise1, local_sem.at[6]),
     ]
+    own_shards = shards.at[pl.ds(grp * WG, WG)]
     tables = [
-        (shard, shards.at[pl.ds(grp * WG, WG)]),
+        (own_shards, own_shards),
         (weights, w_all.at[grp]),
         (copies, c_all.at[grp]),
         (owners, o_all.at[grp]),
     ]
     local += [
-        pltpu.make_async_copy(source, place, local_sem.at[7 + i]) for i, (source, place) in enumerate(tables)
-    ]
-    for copy in starts + local:
+        pltpu.make_async_copy(source, place, local_sem.at[7 + i]) for i, (source, place) in enumerate(tables) if i
+    ]
+    for copy in local:
         copy.start()
     acc[...] = jnp.zeros_like(acc)
-    for copy in starts:
-        copy.wait()
+    load.wait()
+    parts = [jnp.swapaxes(green_v[:, c].astype(F32), 0, 1) for c in range(2)]
+    for c in range(4):
+        row = jnp.concatenate(
+            [parts[i][c][:, h * 64 : h * 64 + 64] for h in range(2) for i in range(2)], 1
+        ).astype(BF16)
+        chunks[c][x, y, z] = row
+        shards[grp * WG + c] = row
     pl.semaphore_wait(barrier, len(everyone))
 
     def remote(source, target, send, recv, where):
@@ -104,42 +110,37 @@
     def move(stream, phase, kind):
         chunk, rows, cols, order = STREAMS[stream]
         axis, free = order[phase], order[:phase]
-        up, down, far = dict(here), dict(here), dict(here)
-        up[axis] = (here[axis] + 1) % 4
-        down[axis] = (here[axis] + 3) % 4
-        far[axis] = (here[axis] + 2) % 4
-        at, to, span = here, (up, down, far)[kind % 3], slice(None)
-        if phase == 2 and kind == 2:
-            at, to, span = down, up, pl.ds(0, 2)
-        if phase == 2 and kind == 3:
-            at, to, span = up, down, pl.ds(2, 2)
-        index = [(span if a == order[0] else slice(None)) if a in free else at[a] for a in "xyz"]
+        to = dict(here)
+        to[axis] = (here[axis] + (1, 3, 2)[kind]) % 4
+        index = [slice(None) if a in free else here[a] for a in "xyz"]
         ref = chunks[chunk].at[(*index, pl.ds(*rows), pl.ds(*cols))]
         return remote(
             ref, ref, send_sem.at[stream, phase, kind], recv_sem.at[stream, phase, kind],
             device(to["x"], to["y"], to["z"], core),
         )
 
-    def begin(stream, phase):
-        for kind in (0, 1) if phase == 2 else (0, 1, 2):
-            move(stream, phase, kind).start()
-
-    def arrive(stream, phase):
-        for kind in range(3):
-            move(stream, phase, kind).wait_recv()
-
-    def forward(stream):
-        move(stream, 2, 0).wait_recv()
-        move(stream, 2, 2).start()
-        move(stream, 2, 1).wait_recv()
-        move(stream, 2, 3).start()
-
-    def finish(stream):
-        move(stream, 2, 2).wait_recv()
-        move(stream, 2, 3).wait_recv()
-        for phase in range(3):
-            for kind in range(4 if phase == 2 else 3):
-                move(stream, phase, kind).wait_send()
+    def streams(chunk):
+        return range(3 * chunk, 3 * chunk + 3)
+
+    def begin(chunk, phase):
+        for s in streams(chunk):
+            for kind in (2, 0, 1):
+                move(s, phase, kind).start()
+
+    def arrive(chunk, phase):
+        for s in streams(chunk):
+            for kind in range(3):
+                move(s, phase, kind).wait_recv()
+
+    def advance(chunk, phase):
+        arrive(chunk, phase - 1)
+        begin(chunk, phase)
+
+    def sent(chunk):
+        for s in streams(chunk):
+            for phase in range(3):
+                for kind in range(3):
+                    move(s, phase, kind).wait_send()
 
     swaps = [
         remote(ids, ids_v, pair_send.at[0], pair_recv.at[0], sibling),
@@ -151,45 +152,49 @@
         for j, (source, place) in enumerate(tables):
             groups.append(remote(source, place, group_send.at[j, i], group_recv.at[j, i], target))
 
-    def streams(chunk):
-        return range(3 * chunk, 3 * chunk + 3)
-
-    def advance(chunk, phase):
-        def run():
-            for s in streams(chunk):
-                arrive(s, phase - 1)
-                begin(s, phase)
-        return run
-
-    def onward(chunk):
-        def run():
-            for s in streams(chunk):
-                forward(s)
-        return run
-
-    def complete(chunk):
-        for s in streams(chunk):
-            finish(s)
-
-    for s in streams(0):
-        begin(s, 0)
+    begin(0, 0)
     for copy in swaps:
         copy.start()
-    advance(0, 1)()
-    advance(0, 2)()
-    for s in streams(1):
-        begin(s, 0)
-    onward(0)()
+    advance(0, 1)
+    advance(0, 2)
+    begin(1, 0)
     swaps[0].wait()
     ids_copy = pltpu.make_async_copy(ids_v, ids_s.at[1], local_sem.at[11])
     ids_copy.start()
     for copy in local:
         copy.wait()
     ids_copy.wait()
-    complete(0)
+    advance(1, 1)
+    arrive(0, 2)
+
+    def later(*steps):
+        def run():
+            for step in steps:
+                step()
+        return run
+
+    def go(chunk, phase):
+        return (lambda: advance(chunk, phase)) if phase else (lambda: begin(chunk, 0))
+
+    events = (
+        {
+            0: later(go(1, 2), go(2, 0)),
+            1: later(go(2, 1)),
+            2: later(lambda: swaps[2].wait(), go(2, 2), go(3, 0)),
+            3: later(go(3, 1)),
+        },
+        {0: later(go(3, 2)), 1: later(*[copy.start for copy in groups])},
+        {},
+        {},
+    )
 
     lane16 = lax.broadcasted_iota(jnp.int32, (16, 128), 1)
-    masks = [(lane16 // 16) == r for r in range(8)]
+    masks = [(lane16 % 64) // 16 == r for r in range(4)]
+    sign = jnp.where(lax.broadcasted_iota(jnp.int32, (64, 128), 1) < 64, -1.0, 1.0).astype(BF16)
+
+    def times_i(block):
+        return pltpu.roll(block, 64, 1) * sign
+
     keep = (lane16 % 16) == lax.broadcasted_iota(jnp.int32, (16, 128), 0)
 
     def compute(chunk, actions):
@@ -204,9 +209,9 @@
                 for j in range(2):
                     b = ids_s[part_of, j, lax.rem(turn, count // STEP) * STEP + k]
                     places.append((lax.rem(lax.div(b, 2), 2), lax.div(b, 4), lax.rem(b, 2) * 2))
+            tees = []
             for xh in range(2):
                 w = xh * 4 + chunk
-                lefts, rights = [], []
                 for k in range(STEP):
                     g = turn * STEP + k
                     rows = [
@@ -216,52 +221,55 @@
                     tee = jnp.dot(
                         vec[g], jnp.concatenate(rows, 0), preferred_element_type=F32
                     ).astype(BF16)
-                    real, imag = tee[:, :128], tee[:, 128:]
-                    diag[w, pl.ds(g, 1)] = diagonal(real, masks, keep)
-                    diag[8 + w, pl.ds(g, 1)] = diagonal(imag, masks, keep)
-                    lefts.append(tee)
-                    rights += [tee, jnp.concatenate([-imag, real], 1)]
-                acc[w] += jnp.dot(
-                    jnp.concatenate(lefts, 1), jnp.concatenate(rights, 0), preferred_element_type=F32
-                )
+                    diag[w, pl.ds(g, 1)] = diagonal(tee[:64, :128], masks, keep)
+                    diag[8 + w, pl.ds(g, 1)] = diagonal(tee[64:, 128:], masks, keep)
+                    tees.append(tee)
+            for xh in range(2):
+                w = xh * 4 + chunk
+                left1, right1, left2, right2 = [], [], [], []
+                for tee in tees[xh * STEP : (xh + 1) * STEP]:
+                    a, b, c, d = tee[:64, :128], tee[:64, 128:], tee[64:, :128], tee[64:, 128:]
+                    left1 += [a, d]
+                    right1 += [a, times_i(a), d, times_i(d)]
+                    left2.append(b)
+                    right2 += [c, times_i(c)]
+                for i, (left, right) in enumerate(((left1, right1), (left2, right2))):
+                    acc[w, i] += jnp.dot(
+                        jnp.concatenate(left, 1), jnp.concatenate(right, 0), preferred_element_type=F32
+                    )
             return carry
 
         lax.fori_loop(0, 2 * count // STEP, step, 0)
 
     for chunk in range(4):
-        actions = {}
-        if chunk < 3:
-            actions = {0: advance(chunk + 1, 1), 1: advance(chunk + 1, 2), 3: onward(chunk + 1)}
-        if chunk == 0:
-            actions[2] = lambda: swaps[2].wait()
-        if chunk == 1:
-            for copy in groups:
-                copy.start()
-        compute(chunk, actions)
-        if chunk < 3:
-            if chunk < 2:
-                for s in streams(chunk + 2):
-                    begin(s, 0)
-            complete(chunk + 1)
+        if chunk:
+            arrive(chunk, 2)
+        compute(chunk, events[chunk])
+    for chunk in range(4):
+        sent(chunk)
 
     row16 = lax.broadcasted_iota(jnp.int32, (16, 128), 0)
     bias = jnp.zeros((16, 2 * count), F32)
+    low16 = lane16 < 64
     for r in range(16):
+        pick = row16 == jnp.where(low16, r % 8, 8 + r % 8)
         bias += lax.dot_general(
-            (row16 == r).astype(BF16), diag[r].astype(BF16),
+            pick.astype(BF16), diag[r].astype(BF16),
             (((1,), (1,)), ((), ())), preferred_element_type=F32,
         )
     bias = 2.0 * bias
     bias1[...] = bias
-    eye = lax.broadcasted_iota(jnp.int32, (128, 128), 0) == lax.broadcasted_iota(jnp.int32, (128, 128), 1)
+    eye = lax.broadcasted_iota(jnp.int32, (64, 128), 0) == (
+        lax.broadcasted_iota(jnp.int32, (64, 128), 1) % 64
+    )
     row8 = lax.broadcasted_iota(jnp.int32, (8, 128), 0)
-    kx = [jnp.zeros((8, 128), F32), jnp.zeros((8, 128), F32)]
+    lane8 = lax.broadcasted_iota(jnp.int32, (8, 128), 1)
+    lines = jnp.zeros((8, 128), F32)
     for w in range(8):
-        for c in range(2):
-            line = jnp.sum(
-                jnp.where(eye, acc[w, :, c * 128 : (c + 1) * 128], 0.0), axis=0, keepdims=True
-            )
-            kx[c] += jnp.where(row8 == w, line, 0.0)
+        square = acc[w, 0] + 2.0 * acc[w, 1]
+        line = jnp.sum(jnp.where(eye, square, 0.0), axis=0, keepdims=True)
+        lines = jnp.where(row8 == w, line, lines)
+    kx = [jnp.where(lane8 < 64, lines, 0.0), jnp.where(lane8 < 64, 0.0, lines)]
     swaps[1].wait()
 
     def fields_of(ref):
@@ -276,7 +284,6 @@
     shift_re, shift_im = -ROOT * re, -ROOT * im
     phase_re = fields * shift_re - 0.5 * (shift_re * shift_re - shift_im * shift_im)
     phase_im = fields * shift_im - shift_re * shift_im
-    lane8 = lax.broadcasted_iota(jnp.int32, (8, 128), 1)
     lane_of = ((row8 // 4) * 2 + core) * 4 + row8 % 4
     result = jnp.zeros((8, 128), F32)
     for i, value in enumerate((energy_re, energy_im, phase_re, phase_im)):
@@ -358,11 +365,12 @@
     moved_ref[...] = moved[:, :WG]
 
 
-def fused(shard, vectors, ids, noise, weights, copies, owners):
+def fused(green, vectors, ids, noise, weights, copies, owners):
     vmem = pl.BlockSpec(memory_space=pltpu.VMEM)
     hbm = pl.BlockSpec(memory_space=pl.ANY)
     shape = jax.ShapeDtypeStruct
     count = vectors.shape[0]
+    block = (green.shape[0], 2 * green.shape[3])
     dma = pltpu.SemaphoreType.DMA
     streams = len(STREAMS)
     I32 = jnp.int32
@@ -373,18 +381,18 @@
             shape((2, WG), F32),
             shape((1, WG), F32),
             shape((1, WG), F32),
-            shape(shard.shape, BF16),
+            shape((WG,) + block, BF16),
         ),
         in_specs=[hbm] * 7,
         out_specs=(vmem,) * 5,
-        scratch_shapes=[pltpu.VMEM((4, 4, 4) + shard.shape[1:], BF16)] * 4
+        scratch_shapes=[pltpu.VMEM((4, 4, 4) + block, BF16)] * 4
         + [
             pltpu.VMEM((2 * count,) + vectors.shape[1:], BF16),
             pltpu.VMEM(ids.shape, I32),
             pltpu.SMEM((2,) + ids.shape, I32),
             pltpu.VMEM(noise.shape, F32),
             pltpu.VMEM(noise.shape, F32),
-            pltpu.VMEM((8, 128, 256), F32),
+            pltpu.VMEM((8, 2, 64, 128), F32),
             pltpu.VMEM((16, 2 * count, 128), F32),
             pltpu.VMEM((8, 128), F32),
             pltpu.VMEM((16, 8, 128), F32),
@@ -392,7 +400,8 @@
             pltpu.VMEM((8, 128), F32),
             pltpu.VMEM((16, 2 * count), F32),
             pltpu.VMEM((16, 2 * count), F32),
-            pltpu.VMEM((GROUPS * WG,) + shard.shape[1:], BF16),
+            pltpu.VMEM(green.shape, BF16),
+            pltpu.VMEM((GROUPS * WG,) + block, BF16),
             pltpu.VMEM((GROUPS, 1, WG), F32),
             pltpu.VMEM((GROUPS, 1, WG), I32),
             pltpu.VMEM((GROUPS, WG, KMAX), I32),
@@ -407,16 +416,39 @@
             collective_id=0, has_side_effects=True, vmem_limit_bytes=63 * MB
         ),
         name="fused_step",
-    )(shard, vectors, ids, noise, weights, copies, owners)
+    )(green, vectors, ids, noise, weights, copies, owners)
+
+
+def outputs_kernel(force, energy, new, moved, green, force_ref, energy_ref, new_ref, moved_ref, green_ref):
+    force_ref[...] = force[...]
+    energy_ref[...] = energy[...]
+    new_ref[...] = new[...]
+    moved_ref[...] = moved[...]
+    wide = green[...].astype(F32)
+    for c in range(2):
+        part = jnp.concatenate([wide[:, :, h * 128 + c * 64 : h * 128 + c * 64 + 64] for h in range(2)], 2)
+        green_ref[:, c] = jnp.swapaxes(part, 0, 1).astype(BF16)
+
+
+def outputs(force, energy, new, moved, green):
+    vmem = pl.BlockSpec(memory_space=pltpu.VMEM)
+    slots, rows, columns = green.shape
+    shape = jax.ShapeDtypeStruct
+    return pl.pallas_call(
+        outputs_kernel,
+        out_shape=tuple(shape(a.shape, a.dtype) for a in (force, energy, new, moved))
+        + (shape((rows, 2, slots, columns // 2), BF16),),
+        in_specs=[vmem] * 5,
+        out_specs=(vmem,) * 5,
+        compiler_params=pltpu.CompilerParams(vmem_limit_bytes=63 * MB),
+        name="outputs",
+    )(force, energy, new, moved, green)
 
 
 def body(green, chol_blocks, block_ids, noise, weights, copies, owners):
-    rows, _, _, electrons = green.shape
-    shard = jnp.transpose(green, (2, 0, 1, 3)).reshape(WG, rows, 2 * electrons)
-    force_bias, energy, new_weights, moved_weights, moved = fused(
-        shard, chol_blocks, block_ids.T, noise, weights.reshape(1, WG), copies.reshape(1, WG), owners
-    )
-    moved_green = jnp.transpose(moved.reshape(WG, rows, 2, electrons), (1, 2, 0, 3))
+    force_bias, energy, new_weights, moved_weights, moved_green = outputs(*fused(
+        green, chol_blocks, block_ids.T, noise, weights.reshape(1, WG), copies.reshape(1, WG), owners
+    ))
     return (force_bias, energy, new_weights.reshape(WG), moved_green, moved_weights.reshape(WG))
 
 

time: 101 us -> 91.7 us (0.908)
  local copies, waits for them, and re-layouts: 7.96 us -> 0 us
    unnamed x4 -> x0, local copies, waits for them, and re-layouts: 4.85 us -> none
    pallas_call x1, Pallas kernels: 91.8 us -> 89.3 us  [fused(): pl.pallas_call(fused_kernel, out_shape=(shape((2, GROUPS * WG, count), F3...]
    reshape x3 -> x0, local copies, waits for them, and re-layouts: 2.22 us -> none  [the longest x2 1.54 us: body(): moved.reshape(WG, rows, 2, electrons)]
    pallas_call x0 -> x1, Pallas kernels: none -> 1.62 us  [outputs(): pl.pallas_call(outputs_kernel, out_shape=tuple((shape(a.shape, a.dtype) f...]
where the time goes in v4:
time: 91.7 us; the launch traced here: 91.6 us
  Pallas kernels  90.9 us (99%)
    pallas_call x1, Pallas kernels, fused(): pl.pallas_call(fused_kernel, out_shape=(shape((2, GROUPS * WG, count), F3...  89.3 us

profile of v4, /device:TPU:1, one launch (start us, length us, event | category | flops | bytes accessed | tf_op | source)
XLA Modules:
  0.0 91.6 jit_solution(12313573421478685222)
XLA Ops:
  0.6 89.3 %fused_step.1 = (f32[2,16,64]{2,1,0:T(8,128)}, f32[2,4]{1,0:T(2,128)}, f32[1,4]{1,0:T(1,128)}, f32[1,4]{1,0:T(1,128)}, bf16[4,32,256]{2,1,0:T(8,128)(2,1)}) custom-call(bf16[32,2,4,128]{3,2,1,0:T(4,128)(2,1)} %green.1, bf16[64,128,128]{2,1,0:T(8,128)(2,1)} %vectors.1, s32[2,64]{1,0:T(2,128)} %bitcast.5, f32[16,64]{1,0:T(8,128)} %noise.1, f32[1,4]{1,0:T(1,128)} %bitcast.6, ...), custom_call_target="tpu_custom_call" | custom-call | tf_op jit(solution)/shard_map/fused_step/pallas_call | solution.py:377
  89.9 1.6 %outputs.1 = (f32[2,16,64]{2,1,0:T(8,128)}, f32[2,4]{1,0:T(2,128)}, f32[1,4]{1,0:T(1,128)}, f32[1,4]{1,0:T(1,128)}, bf16[32,2,4,128]{3,2,1,0:T(4,128)(2,1)}) custom-call(f32[2,16,64]{2,1,0:T(8,128)} %get-tuple-element.15.force, f32[2,4]{1,0:T(2,128)} %get-tuple-element.16.energy, f32[1,4]{1,0:T(1,128)} %get-tuple-element.17.new, ...), custom_call_target="tpu_custom_call" | custom-call | tf_op jit(solution)/shard_map/outputs/pallas_call | solution.py:437

commit v5 on v4

--- a/solution.py
+++ b/solution.py
@@ -157,7 +157,8 @@
         copy.start()
     advance(0, 1)
     advance(0, 2)
-    begin(1, 0)
+    for chunk in (1, 2, 3):
+        begin(chunk, 0)
     swaps[0].wait()
     ids_copy = pltpu.make_async_copy(ids_v, ids_s.at[1], local_sem.at[11])
     ids_copy.start()
@@ -174,17 +175,12 @@
         return run
 
     def go(chunk, phase):
-        return (lambda: advance(chunk, phase)) if phase else (lambda: begin(chunk, 0))
+        return lambda: advance(chunk, phase)
 
     events = (
-        {
-            0: later(go(1, 2), go(2, 0)),
-            1: later(go(2, 1)),
-            2: later(lambda: swaps[2].wait(), go(2, 2), go(3, 0)),
-            3: later(go(3, 1)),
-        },
-        {0: later(go(3, 2)), 1: later(*[copy.start for copy in groups])},
-        {},
+        {0: go(1, 2), 2: lambda: swaps[2].wait(), 3: go(2, 1)},
+        {0: go(2, 2), 1: later(*[copy.start for copy in groups]), 2: go(3, 1)},
+        {0: go(3, 2)},
         {},
     )
 

time: 91.7 us -> 80.8 us (0.88)
  Pallas kernels: 90.9 us -> 80 us
    pallas_call x1, Pallas kernels: 89.3 us -> 78.4 us  [fused(): pl.pallas_call(fused_kernel, out_shape=(shape((2, GROUPS * WG, count), F3...]
where the time goes in v5:
time: 80.8 us; the launch traced here: 80.7 us
  Pallas kernels  80 us (99%)
    pallas_call x1, Pallas kernels, fused(): pl.pallas_call(fused_kernel, out_shape=(shape((2, GROUPS * WG, count), F3...  78.4 us
    pallas_call x1, Pallas kernels, outputs(): pl.pallas_call(outputs_kernel, out_shape=tuple((shape(a.shape, a.dtype) f...  1.62 us

profile of v5, /device:TPU:1, one launch (start us, length us, event | category | flops | bytes accessed | tf_op | source)
XLA Modules:
  0.0 80.7 jit_solution(2111366289636938825)
XLA Ops:
  0.6 78.4 %fused_step.1 = (f32[2,16,64]{2,1,0:T(8,128)}, f32[2,4]{1,0:T(2,128)}, f32[1,4]{1,0:T(1,128)}, f32[1,4]{1,0:T(1,128)}, bf16[4,32,256]{2,1,0:T(8,128)(2,1)}) custom-call(bf16[32,2,4,128]{3,2,1,0:T(4,128)(2,1)} %green.1, bf16[64,128,128]{2,1,0:T(8,128)(2,1)} %vectors.1, s32[2,64]{1,0:T(2,128)} %bitcast.5, f32[16,64]{1,0:T(8,128)} %noise.1, f32[1,4]{1,0:T(1,128)} %bitcast.6, ...), custom_call_target="tpu_custom_call" | custom-call | tf_op jit(solution)/shard_map/fused_step/pallas_call | solution.py:373
  79.0 1.6 %outputs.1 = (f32[2,16,64]{2,1,0:T(8,128)}, f32[2,4]{1,0:T(2,128)}, f32[1,4]{1,0:T(1,128)}, f32[1,4]{1,0:T(1,128)}, bf16[32,2,4,128]{3,2,1,0:T(4,128)(2,1)}) custom-call(f32[2,16,64]{2,1,0:T(8,128)} %get-tuple-element.15.force, f32[2,4]{1,0:T(2,128)} %get-tuple-element.16.energy, f32[1,4]{1,0:T(1,128)} %get-tuple-element.17.new, ...), custom_call_target="tpu_custom_call" | custom-call | tf_op jit(solution)/shard_map/outputs/pallas_call | solution.py:433

commit v6 on v5

--- a/solution.py
+++ b/solution.py
@@ -33,7 +33,7 @@
 STREAMS = tuple(
     (chunk, *WINDOWS[i], ORDERS[(chunk + i) % 3]) for chunk in range(4) for i in range(3)
 )
-STEP = 32
+STEP = 64
 
 
 def diagonal(block, masks, keep):
@@ -178,8 +178,8 @@
         return lambda: advance(chunk, phase)
 
     events = (
-        {0: go(1, 2), 2: lambda: swaps[2].wait(), 3: go(2, 1)},
-        {0: go(2, 2), 1: later(*[copy.start for copy in groups]), 2: go(3, 1)},
+        {0: go(1, 2), 1: later(lambda: swaps[2].wait(), go(2, 1))},
+        {0: go(2, 2), 1: later(*[copy.start for copy in groups], go(3, 1))},
         {0: go(3, 2)},
         {},
     )
@@ -241,9 +241,6 @@
         if chunk:
             arrive(chunk, 2)
         compute(chunk, events[chunk])
-    for chunk in range(4):
-        sent(chunk)
-
     row16 = lax.broadcasted_iota(jnp.int32, (16, 128), 0)
     bias = jnp.zeros((16, 2 * count), F32)
     low16 = lane16 < 64
@@ -299,6 +296,8 @@
         copy.start()
     swap = remote(bias1, bias2, pair_send.at[3], pair_recv.at[3], sibling)
     swap.start()
+    for chunk in range(4):
+        sent(chunk)
     for copy in groups:
         copy.wait()
     scalars = [

time: 80.8 us -> 78.5 us (0.972)
  Pallas kernels: 80 us -> 77.7 us
    pallas_call x1, Pallas kernels: 78.4 us -> 76.1 us  [fused(): pl.pallas_call(fused_kernel, out_shape=(shape((2, GROUPS * WG, count), F3...]
where the time goes in v6:
time: 78.5 us; the launch traced here: 78.3 us
  Pallas kernels  77.7 us (99%)
    pallas_call x1, Pallas kernels, fused(): pl.pallas_call(fused_kernel, out_shape=(shape((2, GROUPS * WG, count), F3...  76.1 us
    pallas_call x1, Pallas kernels, outputs(): pl.pallas_call(outputs_kernel, out_shape=tuple((shape(a.shape, a.dtype) f...  1.62 us

profile of v6, /device:TPU:1, one launch (start us, length us, event | category | flops | bytes accessed | tf_op | source)
XLA Modules:
  0.0 78.3 jit_solution(12010860253531615242)
XLA Ops:
  0.6 76.1 %fused_step.1 = (f32[2,16,64]{2,1,0:T(8,128)}, f32[2,4]{1,0:T(2,128)}, f32[1,4]{1,0:T(1,128)}, f32[1,4]{1,0:T(1,128)}, bf16[4,32,256]{2,1,0:T(8,128)(2,1)}) custom-call(bf16[32,2,4,128]{3,2,1,0:T(4,128)(2,1)} %green.1, bf16[64,128,128]{2,1,0:T(8,128)(2,1)} %vectors.1, s32[2,64]{1,0:T(2,128)} %bitcast.5, f32[16,64]{1,0:T(8,128)} %noise.1, f32[1,4]{1,0:T(1,128)} %bitcast.6, ...), custom_call_target="tpu_custom_call" | custom-call | tf_op jit(solution)/shard_map/fused_step/pallas_call | solution.py:372
  76.7 1.6 %outputs.1 = (f32[2,16,64]{2,1,0:T(8,128)}, f32[2,4]{1,0:T(2,128)}, f32[1,4]{1,0:T(1,128)}, f32[1,4]{1,0:T(1,128)}, bf16[32,2,4,128]{3,2,1,0:T(4,128)(2,1)}) custom-call(f32[2,16,64]{2,1,0:T(8,128)} %get-tuple-element.15.force, f32[2,4]{1,0:T(2,128)} %get-tuple-element.16.energy, f32[1,4]{1,0:T(1,128)} %get-tuple-element.17.new, ...), custom_call_target="tpu_custom_call" | custom-call | tf_op jit(solution)/shard_map/outputs/pallas_call | solution.py:432

commit v7 on v6

--- a/solution.py
+++ b/solution.py
@@ -46,10 +46,10 @@
 def fused_kernel(
     green, vectors, ids, noise, weights, copies, owners,
     force_ref, energy_ref, new_ref, moved_ref, green_ref,
-    g0, g1, g2, g3, vec, ids_v, ids_s, noise1, noise2, acc, diag, part, slots, slots2, own2,
+    g0, g1, g2, g3, vec, ids_v, ids_s, noise1, noise2, acc, diag, part, rounds,
     bias1, bias2, green_v, shards, w_all, c_all, o_all, w_s, c_s, o_s,
     local_sem, send_sem, recv_sem, pair_send, pair_recv, group_send, group_recv,
-    send1, recv1, send2, recv2,
+    send1, recv1,
 ):
     chunks = (g0, g1, g2, g3)
     x, y, z, core = position()
@@ -58,15 +58,13 @@
     here = {"x": x, "y": y, "z": z}
     sibling = device(x, y, z, 1 - core)
     across = [device((x + 2) % 4, y, z, core), device((x + 2) % 4, y, z, 1 - core)]
-    plane = [
-        device((x + i) % 4, (y + j) % 4, z, core)
-        for i in range(4) for j in range(4) if i + j > 0
-    ]
     column = [
         device(x, y, (z + i) % 4, (core + k) % 2)
         for k in range(2) for i in range(4) if i + k > 0
     ]
-    everyone = plane + column + [across[1]]
+    everyone = column + [across[1]]
+    everyone += [device((x + i) % 4, y, z, core) for i in (1, 2, 3)]
+    everyone += [device(x, (y + i) % 4, z, core) for i in (1, 2, 3)]
     barrier = pltpu.get_barrier_semaphore()
     for target in everyone:
         pl.semaphore_signal(barrier, inc=1, device_id=target, device_id_type=MESH)
@@ -136,9 +134,9 @@
         arrive(chunk, phase - 1)
         begin(chunk, phase)
 
-    def sent(chunk):
+    def sent(chunk, phases):
         for s in streams(chunk):
-            for phase in range(3):
+            for phase in phases:
                 for kind in range(3):
                     move(s, phase, kind).wait_send()
 
@@ -157,16 +155,18 @@
         copy.start()
     advance(0, 1)
     advance(0, 2)
-    for chunk in (1, 2, 3):
-        begin(chunk, 0)
+    begin(1, 0)
     swaps[0].wait()
     ids_copy = pltpu.make_async_copy(ids_v, ids_s.at[1], local_sem.at[11])
     ids_copy.start()
     for copy in local:
         copy.wait()
     ids_copy.wait()
+    sent(0, (0, 1))
     advance(1, 1)
     arrive(0, 2)
+    begin(2, 0)
+    begin(3, 0)
 
     def later(*steps):
         def run():
@@ -283,21 +283,22 @@
         column_sum = jnp.sum(value, axis=1, keepdims=True)
         line = jnp.sum(jnp.where(lane8 == lane_of, column_sum, 0.0), axis=0, keepdims=True)
         result = jnp.where(row8 == i, line, result)
-    part[...] = result
-
-    me = x * 4 + y
-    me2 = core * 4 + z
-    slots[me] = result
-    round1 = [
-        remote(part, slots.at[me], send1.at[i], recv1.at[i], target)
-        for i, target in enumerate(plane)
-    ]
-    for copy in round1:
-        copy.start()
+    def exchange(phase, targets, place, value):
+        rounds[phase, place] = value
+        part[phase] = value
+        copies_out = [
+            remote(part.at[phase], rounds.at[phase, place], send1.at[phase, i], recv1.at[phase, i], target)
+            for i, target in enumerate(targets)
+        ]
+        for copy in copies_out:
+            copy.start()
+        return copies_out
+
+    ring_x = [device((x + i) % 4, y, z, core) for i in (2, 1, 3)]
+    ring_y = [device(x, (y + i) % 4, z, core) for i in (2, 1, 3)]
+    round1 = exchange(0, ring_x, x, result)
     swap = remote(bias1, bias2, pair_send.at[3], pair_recv.at[3], sibling)
     swap.start()
-    for chunk in range(4):
-        sent(chunk)
     for copy in groups:
         copy.wait()
     scalars = [
@@ -325,15 +326,13 @@
 
     for copy in round1:
         copy.wait()
-    mine = jnp.sum(slots[...], axis=0)
-    own2[...] = mine
-    slots2[me2] = mine
-    round2 = [
-        remote(own2, slots2.at[me2], send2.at[i], recv2.at[i], target)
-        for i, target in enumerate(column)
-    ]
+    round2 = exchange(1, ring_y, y, jnp.sum(rounds[0, 0:4], axis=0))
     for copy in round2:
-        copy.start()
+        copy.wait()
+    round3 = exchange(2, column, core * 4 + z, jnp.sum(rounds[1, 0:4], axis=0))
+    sent(0, (2,))
+    for chunk in range(1, 4):
+        sent(chunk, range(3))
     swap.wait()
     theirs = pltpu.roll(bias2[...], 64, 1)[:, :count]
     ours = bias[:, :count]
@@ -344,9 +343,9 @@
             force_ref[c, xh * 8 : xh * 8 + 8] = jnp.concatenate(
                 [jnp.where(core == 0, one, two), jnp.where(core == 0, two, one)], 0
             )
-    for copy in round2:
-        copy.wait()
-    total = jnp.sum(slots2[...], axis=0)
+    for copy in round3:
+        copy.wait()
+    total = jnp.sum(rounds[2], axis=0)
     new = weight_line * jnp.exp(total[2:3]) * jnp.maximum(jnp.cos(total[3:4]), 0.0)
     moved = jnp.zeros((1, 128), F32)
     for s in range(WG):
@@ -389,10 +388,8 @@
             pltpu.VMEM(noise.shape, F32),
             pltpu.VMEM((8, 2, 64, 128), F32),
             pltpu.VMEM((16, 2 * count, 128), F32),
-            pltpu.VMEM((8, 128), F32),
-            pltpu.VMEM((16, 8, 128), F32),
-            pltpu.VMEM((8, 8, 128), F32),
-            pltpu.VMEM((8, 128), F32),
+            pltpu.VMEM((3, 8, 128), F32),
+            pltpu.VMEM((3, 8, 8, 128), F32),
             pltpu.VMEM((16, 2 * count), F32),
             pltpu.VMEM((16, 2 * count), F32),
             pltpu.VMEM(green.shape, BF16),
@@ -405,7 +402,7 @@
             pltpu.SMEM((GROUPS, WG, KMAX), I32),
             dma((15,)), dma((streams, 3, 4)), dma((streams, 3, 4)),
             dma((4,)), dma((4,)), dma((4, 3)), dma((4, 3)),
-            dma((15,)), dma((15,)), dma((7,)), dma((7,)),
+            dma((3, 7)), dma((3, 7)),
         ],
         compiler_params=pltpu.CompilerParams(
             collective_id=0, has_side_effects=True, vmem_limit_bytes=63 * MB

time: 78.5 us -> 77.2 us (0.983)
  Pallas kernels: 77.7 us -> 76.4 us
    pallas_call x1, Pallas kernels: 76.1 us -> 74.7 us  [fused(): pl.pallas_call(fused_kernel, out_shape=(shape((2, GROUPS * WG, count), F3...]
where the time goes in v7:
time: 77.2 us; the launch traced here: 77 us
  Pallas kernels  76.4 us (99%)
    pallas_call x1, Pallas kernels, fused(): pl.pallas_call(fused_kernel, out_shape=(shape((2, GROUPS * WG, count), F3...  74.7 us
    pallas_call x1, Pallas kernels, outputs(): pl.pallas_call(outputs_kernel, out_shape=tuple((shape(a.shape, a.dtype) f...  1.62 us

profile of v7, /device:TPU:1, one launch (start us, length us, event | category | flops | bytes accessed | tf_op | source)
XLA Modules:
  0.0 77.0 jit_solution(10062453254538294531)
XLA Ops:
  0.6 74.7 %fused_step.1 = (f32[2,16,64]{2,1,0:T(8,128)}, f32[2,4]{1,0:T(2,128)}, f32[1,4]{1,0:T(1,128)}, f32[1,4]{1,0:T(1,128)}, bf16[4,32,256]{2,1,0:T(8,128)(2,1)}) custom-call(bf16[32,2,4,128]{3,2,1,0:T(4,128)(2,1)} %green.1, bf16[64,128,128]{2,1,0:T(8,128)(2,1)} %vectors.1, s32[2,64]{1,0:T(2,128)} %bitcast.5, f32[16,64]{1,0:T(8,128)} %noise.1, f32[1,4]{1,0:T(1,128)} %bitcast.6, ...), custom_call_target="tpu_custom_call" | custom-call | tf_op jit(solution)/shard_map/fused_step/pallas_call | solution.py:371
  75.4 1.6 %outputs.1 = (f32[2,16,64]{2,1,0:T(8,128)}, f32[2,4]{1,0:T(2,128)}, f32[1,4]{1,0:T(1,128)}, f32[1,4]{1,0:T(1,128)}, bf16[32,2,4,128]{3,2,1,0:T(4,128)(2,1)}) custom-call(f32[2,16,64]{2,1,0:T(8,128)} %get-tuple-element.15.force, f32[2,4]{1,0:T(2,128)} %get-tuple-element.16.energy, f32[1,4]{1,0:T(1,128)} %get-tuple-element.17.new, ...), custom_call_target="tpu_custom_call" | custom-call | tf_op jit(solution)/shard_map/outputs/pallas_call | solution.py:429

commit v8 on v7

--- a/solution.py
+++ b/solution.py
@@ -156,6 +156,8 @@
     advance(0, 1)
     advance(0, 2)
     begin(1, 0)
+    for copy in groups:
+        copy.start()
     swaps[0].wait()
     ids_copy = pltpu.make_async_copy(ids_v, ids_s.at[1], local_sem.at[11])
     ids_copy.start()
@@ -179,7 +181,7 @@
 
     events = (
         {0: go(1, 2), 1: later(lambda: swaps[2].wait(), go(2, 1))},
-        {0: go(2, 2), 1: later(*[copy.start for copy in groups], go(3, 1))},
+        {0: go(2, 2), 1: go(3, 1)},
         {0: go(3, 2)},
         {},
     )

time: 77.2 us -> 76.3 us (0.988)
  Pallas kernels: 76.4 us -> 75.4 us
    pallas_call x1, Pallas kernels: 74.7 us -> 73.8 us  [fused(): pl.pallas_call(fused_kernel, out_shape=(shape((2, GROUPS * WG, count), F3...]
where the time goes in v8:
time: 76.3 us; the launch traced here: 76.1 us
  Pallas kernels  75.4 us (99%)
    pallas_call x1, Pallas kernels, fused(): pl.pallas_call(fused_kernel, out_shape=(shape((2, GROUPS * WG, count), F3...  73.8 us
    pallas_call x1, Pallas kernels, outputs(): pl.pallas_call(outputs_kernel, out_shape=tuple((shape(a.shape, a.dtype) f...  1.62 us

profile of v8, /device:TPU:1, one launch (start us, length us, event | category | flops | bytes accessed | tf_op | source)
XLA Modules:
  0.0 76.1 jit_solution(11489772438895019411)
XLA Ops:
  0.6 73.8 %fused_step.1 = (f32[2,16,64]{2,1,0:T(8,128)}, f32[2,4]{1,0:T(2,128)}, f32[1,4]{1,0:T(1,128)}, f32[1,4]{1,0:T(1,128)}, bf16[4,32,256]{2,1,0:T(8,128)(2,1)}) custom-call(bf16[32,2,4,128]{3,2,1,0:T(4,128)(2,1)} %green.1, bf16[64,128,128]{2,1,0:T(8,128)(2,1)} %vectors.1, s32[2,64]{1,0:T(2,128)} %bitcast.5, f32[16,64]{1,0:T(8,128)} %noise.1, f32[1,4]{1,0:T(1,128)} %bitcast.6, ...), custom_call_target="tpu_custom_call" | custom-call | tf_op jit(solution)/shard_map/fused_step/pallas_call | solution.py:373
  74.5 1.6 %outputs.1 = (f32[2,16,64]{2,1,0:T(8,128)}, f32[2,4]{1,0:T(2,128)}, f32[1,4]{1,0:T(1,128)}, f32[1,4]{1,0:T(1,128)}, bf16[32,2,4,128]{3,2,1,0:T(4,128)(2,1)}) custom-call(f32[2,16,64]{2,1,0:T(8,128)} %get-tuple-element.15.force, f32[2,4]{1,0:T(2,128)} %get-tuple-element.16.energy, f32[1,4]{1,0:T(1,128)} %get-tuple-element.17.new, ...), custom_call_target="tpu_custom_call" | custom-call | tf_op jit(solution)/shard_map/outputs/pallas_call | solution.py:431
